TPU v7x, 128 devices: a whole 4x4x4 slice. The times are simulated.
128 devices in a mesh: fsdp: 16 (over y, x_hi, core), roll: 8 (over z, x_lo).
Axes of the slice: x: 4 (x_hi: 2, x_lo: 2; x = x_hi * 2 + x_lo), y: 4, z: 4, core: 2. Of those that a mesh axis runs over, the one named last changes fastest.
Arguments:
- activations: bfloat16 [16384, 5120], P('fsdp'), may hold values from -6 to 6
- cotangent: bfloat16 [16384, 5120], P('fsdp', 'roll'), may hold values from -0.125 to 0.125
- first_moment: float32 [5120, 5120], P('fsdp', 'roll'), may hold values from -4 to 4
- second_moment: float32 [5120, 5120], P('fsdp', 'roll'), may hold values from 0.05 to 5
- sketch: float32 [5120, 128], P('roll'), may hold values from -0.078125 to 0.078125
Outputs:
- new_first: float32 [5120, 5120], P('fsdp', 'roll')
- new_second: float32 [5120, 5120], P('fsdp', 'roll')
- rebuilt: bfloat16 [5120, 5120], P('roll')
All inputs are finite; a program needn't handle non-finite values.
Results may differ from a plain program's by a relative error of at most 0.006.
Values may be sent and summed in bfloat16 or wider, within the bound.
A program may use at most 192 MiB of HBM per device.

v0:
```python
import jax
import jax.numpy as jnp
from jax import lax
from jax.sharding import PartitionSpec as P

beta_one = 0.9
beta_two = 0.95
epsilon = 1e-08
hp = lax.Precision.HIGHEST


def local(activations, cotangent, first_moment, second_moment, sketch):
    own_cols = first_moment.shape[1]
    grad = lax.psum_scatter(
        lax.dot_general(
            activations, cotangent, (((0,), (0,)), ((), ())), preferred_element_type=jnp.float32
        ),
        "fsdp",
        scatter_dimension=0,
        tiled=True,
    )
    new_first = beta_one * first_moment + (1.0 - beta_one) * grad
    new_second = beta_two * second_moment + (1.0 - beta_two) * grad * grad
    direction = (
        new_first / (1.0 - beta_one**20) / (jnp.sqrt(new_second / (1.0 - beta_two**20)) + epsilon)
    )
    sketched = lax.psum(jnp.dot(direction, sketch, precision=hp), "roll")
    gram = lax.psum(jnp.dot(sketched.T, sketched, precision=hp), "fsdp")
    lower = jnp.linalg.cholesky(gram)
    basis = lax.linalg.triangular_solve(lower, sketched.T, left_side=True, lower=True).T
    coeffs = lax.psum(jnp.dot(basis.T, direction, precision=hp), "fsdp")
    basis_low = basis.astype(jnp.bfloat16)
    coeffs_low = coeffs.astype(jnp.bfloat16)
    all_basis = lax.all_gather(basis_low, "fsdp", axis=0, tiled=True)
    engine_rows = lax.dynamic_slice_in_dim(
        all_basis, lax.axis_index("roll") * own_cols, own_cols, 0
    )
    rebuilt = jnp.dot(
        engine_rows,
        lax.all_gather(coeffs_low, "roll", axis=1, tiled=True),
        preferred_element_type=jnp.float32,
    ).astype(jnp.bfloat16)
    return (new_first, new_second, rebuilt)


def solution(mesh):
    placed = (
        P("fsdp", None),
        P("fsdp", "roll"),
        P("fsdp", "roll"),
        P("fsdp", "roll"),
        P("roll", None),
    )
    return jax.shard_map(
        local,
        mesh=mesh,
        in_specs=placed,
        out_specs=(P("fsdp", "roll"), P("fsdp", "roll"), P("roll", None)),
        check_vma=False,
    )
```

profile of v0, /device:TPU:1, one launch (start us, length us, event | category | flops | bytes accessed | tf_op | source)
XLA Modules:
  0.0 553.2 jit_solution(17710808408314104238)
XLA Ops:
  7.2 1.3 copy-done
  8.5 13.8 %fusion.9 = f32[5120,640]{1,0:T(8,128)} fusion(bf16[1024,5120]{1,0:T(8,128)(2,1)} %param.5, bf16[1024,640]{1,0:T(8,128)(2,1)S(1)} %copy-done), kind=kOutput, calls=%fused_computation.20 | convolution fusion | flops 6710886400 | bytes 24903680 | tf_op jit(solution)/shard_map/dot_general | solution.py:15
  22.4 127.3 %reduce-scatter.2.cloned.1.call-done = f32[320,640]{1,0:T(8,128)} async-done(((f32[5120,640]{1,0:T(8,128)}), f32[320,640]{1,0:T(8,128)}) %reduce-scatter.2.cloned.1.call-update) | async-done | bytes 819216 | tf_op jit(solution)/shard_map/reduce_scatter | solution.py:14
  149.7 1.4 fusion
  151.1 0.9 copy-done.3
  152.0 0.3 copy-done.5
  152.3 1.9 fusion.8
  154.2 66.7 %all-reduce.4.cloned.1.call-done = f32[320,128]{1,0:T(8,128)} async-done(((f32[320,128]{1,0:T(8,128)}), f32[320,128]{1,0:T(8,128)}) %all-reduce.4.cloned.1.call-update) | async-done | bytes 163856 | tf_op jit(solution)/shard_map/psum | solution.py:27
  220.9 2.1 fusion.10
  223.1 0.2 all-gather.5.cloned.1.call-start
  223.3 130.5 %all-reduce.6.cloned.1.call-done = f32[128,128]{0,1:T(8,128)} async-done(((f32[128,128]{0,1:T(8,128)}), f32[128,128]{0,1:T(8,128)}) %all-reduce.6.cloned.1.call-update) | async-done | bytes 65552 | tf_op jit(solution)/shard_map/psum | solution.py:28
  353.8 0.9 copy.9
  354.7 0.9 fusion.5
  355.6 11.7 %cholesky.16 = f32[128,128]{1,0:T(8,128)S(1)} custom-call(f32[128,128]{1,0:T(8,128)S(1)} %fusion.5), custom_call_target="Cholesky" | custom-call | tf_op jit(solution)/shard_map/jit(cholesky)/cholesky | solution.py:29
  367.3 0.6 compare_reduce_fusion
  368.0 0.7 fusion.2
  368.6 9.8 %custom-call.6 = f32[1,128,128]{1,2,0:T(8,128)S(1)} custom-call(f32[1,128,128]{2,1,0:T(8,128)S(1)} %fusion.2), custom_call_target="InvertDiagBlocksLowerTriangular" | custom-call | tf_op jit(solution)/shard_map/triangular_solve | solution.py:30
  378.5 1.2 fusion.3
  379.7 2.4 fusion.7
  382.1 66.9 %all-reduce.7 = bf16[128,640]{1,0:T(8,128)(2,1)} all-reduce(f32[128,640]{1,0:T(8,128)S(1)} %fusion.7), channel_id=1, replica_groups=mesh['fsdp'=16,'roll'=8] {'fsdp'}, use_global_device_ids=true, to_apply=%region_5.6 | all-reduce | flops 81920 | bytes 491520 | tf_op jit(solution)/shard_map/psum | solution.py:31
  449.1 0.6 convert_bitcast_fusion
  449.7 40.0 %all-gather.5.cloned.1.call-done = bf16[128,5120]{1,0:T(8,128)(2,1)} async-done(((bf16[128,640]{1,0:T(8,128)(2,1)}), bf16[128,5120]{1,0:T(8,128)(2,1)}) %all-gather.5.cloned.1.call-update) | async-done | bytes 1310736 | tf_op jit(solution)/shard_map/all_gather | solution.py:40
  489.8 50.8 %all-gather.3.cloned.1.call-done = bf16[5120,128]{1,0:T(8,128)(2,1)} async-done(((bf16[320,128]{1,0:T(8,128)(2,1)}), bf16[5120,128]{1,0:T(8,128)(2,1)}) %all-gather.3.cloned.1.call-update) | async-done | bytes 1310736 | tf_op jit(solution)/shard_map/all_gather | solution.py:34
  540.6 6.1 %convolution_convert_fusion = bf16[640,5120]{1,0:T(8,128)(2,1)} fusion(bf16[128,5120]{1,0:T(8,128)(2,1)} %all-gather.5.cloned.1.call-done, bf16[5120,128]{1,0:T(8,128)(2,1)} %all-gather.3.cloned.1.call-done, s32[]{:T(128)S(6)} %select_n.8), kind=kOutput, calls=%fused_computation | convolution fusion | flops 842137600 | bytes 8028164 | tf_op jit(solution)/shard_map/dot_general | solution.py:38
  (21 shorter events, 0.3 us)
Async XLA Ops:
  7.2 1.3 copy-start
  7.2 142.5 %reduce-scatter.2.cloned.1.call-start = ((), (), s32[]{:S(2)}) async-start(), calls=%async_computation.1 | async-start | bytes 13926400 | tf_op jit(solution)/shard_map/reduce_scatter | solution.py:14
  22.3 127.4 %copy-start.1 = (f32[320,640]{1,0:T(8,128)S(1)}, f32[320,640]{1,0:T(8,128)}, u32[]{:S(2)}) copy-start(f32[320,640]{1,0:T(8,128)} %param.8) | copy-start | bytes 2457604
  22.3 127.4 %copy-start.2 = (f32[320,640]{1,0:T(8,128)S(1)}, f32[320,640]{1,0:T(8,128)}, u32[]{:S(2)}) copy-start(f32[320,640]{1,0:T(8,128)} %param.7) | copy-start | bytes 2457604
  22.3 129.9 %copy-start.6 = (f32[640,128]{1,0:T(8,128)S(1)}, f32[640,128]{1,0:T(8,128)}, u32[]{:S(2)}) copy-start(f32[640,128]{1,0:T(8,128)} %param.9) | copy-start | bytes 983044
  22.3 198.6 %all-reduce.4.cloned.1.call-start = ((), (), s32[]{:S(2)}) async-start(), calls=%async_computation.2 | async-start | bytes 327680 | tf_op jit(solution)/shard_map/psum | solution.py:27
  151.1 0.9 copy-start.3
  151.1 1.2 copy-start.5
  154.2 225.5 %copy-start.4 = (f32[320,640]{1,0:T(8,128)S(1)}, f32[320,640]{1,0:T(8,128)}, u32[]{:S(2)}) copy-start(f32[320,640]{1,0:T(8,128)} %copy-done.3) | copy-start | bytes 2457604
  154.2 199.6 %all-reduce.6.cloned.1.call-start = ((), (), s32[]{:S(2)}) async-start(), calls=%async_computation.3 | async-start | bytes 131072 | tf_op jit(solution)/shard_map/psum | solution.py:28
  223.1 266.7 %all-gather.5.cloned.1.call-start = ((), (), s32[]{:S(2)}) async-start(), calls=%async_computation.5 | async-start | bytes 1474560 | tf_op jit(solution)/shard_map/all_gather | solution.py:40
  449.0 91.6 %all-gather.3.cloned.1.call-start = ((), (), s32[]{:S(2)}) async-start(), calls=%async_computation.4 | async-start | bytes 1392640 | tf_op jit(solution)/shard_map/all_gather | solution.py:34
Sparse Core Ops, SparseCore 0:
  22.4 127.2 reduce-scatter.1
  154.3 66.5 all-reduce.3
  224.0 129.7 all-reduce.5
  449.1 40.5 all-gather.4
  492.4 48.1 all-gather.2
where the time goes:
time: 554 us; the launch traced here: 553 us
  waiting for transfers between devices  415 us (75%)
  blocking collectives  66.9 us (12%)
  matrix products  27.5 us (5%)
  other arithmetic  25.7 us (5%)
  between operations  13.9 us (3%)
    psum x1, waiting for transfers between devices, local(): gram = lax.psum(jnp.dot(sketched.T, sketched, precision=hp), 'fsdp')  130 us
    reduce_scatter x1, waiting for transfers between devices, local(): lax.psum_scatter(lax.dot_general(activations, cotangent, (((0,), (0,)), (...  127 us
    psum x1, blocking collectives, local(): coeffs = lax.psum(jnp.dot(basis.T, direction, precision=hp), 'fsdp')  66.9 us
    psum x1, waiting for transfers between devices, local(): sketched = lax.psum(jnp.dot(direction, sketch, precision=hp), 'roll')  66.7 us
    all_gather x1, waiting for transfers between devices, local(): all_basis = lax.all_gather(basis_low, 'fsdp', axis=0, tiled=True)  50.8 us
    all_gather x1, waiting for transfers between devices, local(): lax.all_gather(coeffs_low, 'roll', axis=1, tiled=True)  40 us
    dot_general x1, matrix products, local(): lax.dot_general(activations, cotangent, (((0,), (0,)), ((), ())), preferr...  13.8 us
    another operation x3, other arithmetic, local(): lower = jnp.linalg.cholesky(gram)  12.4 us
  transfers between devices with their start and end apart: 5, of which 5 were waited for; matrix products, arithmetic and copies ran while one was open for 0% of the time, Pallas kernels for 0%

commit v1 on v0

v1 whole, which is shorter than its diff:
```python
import functools

import jax
import jax.numpy as jnp
from jax import lax
from jax.experimental import pallas as pl
from jax.experimental.pallas import tpu as pltpu
from jax.sharding import PartitionSpec as P

beta_one = 0.9
beta_two = 0.95
epsilon = 1e-08
hp = lax.Precision.HIGHEST
MESH = pl.DeviceIdType.MESH
f32, bf16 = jnp.float32, jnp.bfloat16
DN0 = (((0,), (0,)), ((), ()))

D, TOK, RANK = 5120, 1024, 128
COLS = 640
ROWS = 320
HALF = 160
PIECE = ROWS // 8

ORDER = ((2, 1), (2, 0), (1, 1), (3, 1), (1, 0), (3, 0), (0, 1), (0, 0))
SEMS = 96


def looped(total, step, body):
    def one(i, carry):
        body(pl.multiple_of(i * step, step))
        return carry
    lax.fori_loop(0, total // step, one, 0)


def kernel(
    act, cot, first, second, sketch,
    new_first, new_second, gram_out, s_out, r_out,
    abuf, cbuf, pbuf, own, psend, crecv, ysend, y1recv, y2recv, xsend, xrecv,
    mbuf, vbuf, dbuf, skbuf, rpart, rrecv, rfull, gpart, gcrecv, gslots, ghalf,
    spart, screcv, sslots,
    lsem, ssem, rsem,
):
    f, r = lax.axis_index("fsdp"), lax.axis_index("roll")
    y, xh, c = f // 4, (f // 2) % 2, f % 2
    z, xl = r // 2, r % 2
    q = f // 2

    def dev(y=y, xh=xh, c=c, z=z, xl=xl):
        return {"fsdp": (y * 2 + xh) * 2 + c, "roll": z * 2 + xl}

    sibling = dev(c=1 - c)
    plus, minus = dev(y=(y + 1) % 4), dev(y=(y + 3) % 4)
    across = dev(xh=1 - xh)

    def chip(k):
        other = (q + k) % 8
        return {"fsdp": other * 2 + c, "roll": r}, other

    def roller(k):
        other = (r + k) % 8
        return {"fsdp": f, "roll": other}, other

    def around_x(k):
        other = (xh * 2 + xl + k) % 4
        return dev(xh=other // 2, xl=other % 2)

    used = [0]

    def remote(src, dst, where):
        i = used[0]
        used[0] += 1
        return pltpu.make_async_remote_copy(
            src_ref=src, dst_ref=dst, send_sem=ssem.at[i], recv_sem=rsem.at[i],
            device_id=where, device_id_type=MESH,
        )

    pending = []

    def send(src, dst, where):
        copy = remote(src, dst, where)
        copy.start()
        pending.append(copy)
        return copy

    loads = []
    c_load = pltpu.make_async_copy(cot, cbuf, lsem.at[8])
    c_load.start()
    for k, (dy, dxh) in enumerate(ORDER):
        block = ((y + dy) % 4) * 2 + (xh + dxh) % 2
        load = pltpu.make_async_copy(
            act.at[:, pl.ds(pl.multiple_of(block * 640, 640), 640)], abuf.at[k], lsem.at[k]
        )
        load.start()
        loads.append(load)
    late = [
        pltpu.make_async_copy(first, mbuf, lsem.at[9]),
        pltpu.make_async_copy(second, vbuf, lsem.at[10]),
        pltpu.make_async_copy(sketch, skbuf, lsem.at[11]),
    ]
    for load in late:
        load.start()

    barrier = pltpu.get_barrier_semaphore()
    greeted = [sibling] + [chip(k)[0] for k in range(1, 8)] + [roller(k)[0] for k in range(1, 8)] + [dev(xh=1 - xh, xl=1 - xl)]
    for other in greeted:
        pl.semaphore_signal(barrier, inc=1, device_id=other, device_id_type=MESH)
    c_load.wait()

    mine = pl.multiple_of(c * ROWS, ROWS)
    theirs = pl.multiple_of((1 - c) * ROWS, ROWS)
    halves = []

    def compute(k):
        loads[k].wait()
        pbuf[...] = lax.dot_general(abuf[k], cbuf[...], DN0, preferred_element_type=f32)

        def split(o):
            psend[k, pl.ds(o, 32)] = pbuf[pl.ds(theirs + o, 32)].astype(bf16)
            own[k, pl.ds(o, 32)] = pbuf[pl.ds(mine + o, 32)]
        looped(ROWS, 32, split)
        if k == 0:
            pl.semaphore_wait(barrier, len(greeted))
        halves.append(send(psend.at[k], crecv.at[k], sibling))

    step_one, step_two = {}, {}

    def post(k):
        dy, dxh = ORDER[k]
        halves[k].wait_recv()
        if dy == 2:
            def add(o):
                ysend[k, pl.ds(o, 32)] = (own[k, pl.ds(o, 32)] + crecv[k, pl.ds(o, 32)].astype(f32)).astype(bf16)
            looped(ROWS, 32, add)
            for way, where in enumerate((plus, minus)):
                step_one[way, dxh] = send(
                    ysend.at[k, pl.ds(way * HALF, HALF)], y1recv.at[way, dxh], where)
        elif dy == 0:
            def add(o):
                own[k, pl.ds(o, 32)] = own[k, pl.ds(o, 32)] + crecv[k, pl.ds(o, 32)].astype(f32)
            looped(ROWS, 32, add)
        else:
            way = 0 if dy == 1 else 1
            alone = (1 - way) * HALF

            def add(o):
                ysend[k, pl.ds(alone + o, 32)] = (
                    own[k, pl.ds(alone + o, 32)] + crecv[k, pl.ds(alone + o, 32)].astype(f32)).astype(bf16)
            looped(HALF, 32, add)
            step_two[way, dxh, 1] = send(
                ysend.at[k, pl.ds(alone, HALF)], y2recv.at[way, dxh, pl.ds(alone, HALF)],
                plus if way == 0 else minus)

    def accumulate(dxh):
        for way, dy in ((0, 1), (1, 3)):
            k = ORDER.index((dy, dxh))
            step_one[way, dxh].wait_recv()
            start = way * HALF

            def add(o):
                ysend[k, pl.ds(start + o, 32)] = (
                    own[k, pl.ds(start + o, 32)] + crecv[k, pl.ds(start + o, 32)].astype(f32)
                    + y1recv[way, dxh, pl.ds(o, 32)].astype(f32)).astype(bf16)
            looped(HALF, 32, add)
            step_two[way, dxh, 0] = send(
                ysend.at[k, pl.ds(start, HALF)], y2recv.at[way, dxh, pl.ds(start, HALF)],
                plus if way == 0 else minus)

    for k in range(8):
        compute(k)
        if k >= 1:
            post(k - 1)
        if k == 6:
            accumulate(1)
    post(7)
    accumulate(0)

    crossing = []
    for part in range(2):
        o0 = part * HALF
        for way in range(2):
            step_two[way, 1, 0 if way == part else 1].wait_recv()

        def add(o):
            at = pl.ds(o0 + o, 32)
            xsend[at] = (own[6, at] + y2recv[0, 1, at].astype(f32) + y2recv[1, 1, at].astype(f32)).astype(bf16)
        looped(HALF, 32, add)
        crossing.append(send(xsend.at[pl.ds(o0, HALF)], xrecv.at[pl.ds(o0, HALF)], across))
    for load in late:
        load.wait()
    stores = []
    for part in range(2):
        o0 = part * HALF
        for way in range(2):
            step_two[way, 0, 0 if way == part else 1].wait_recv()
        crossing[part].wait_recv()

        def adam(o):
            at = pl.ds(o0 + o, 16)
            grad = (own[7, at] + y2recv[0, 0, at].astype(f32) + y2recv[1, 0, at].astype(f32)
                    + xrecv[at].astype(f32))
            new_m = beta_one * mbuf[at] + (1.0 - beta_one) * grad
            new_v = beta_two * vbuf[at] + (1.0 - beta_two) * grad * grad
            mbuf[at] = new_m
            vbuf[at] = new_v
            dbuf[at] = new_m / (1.0 - beta_one**20) / (jnp.sqrt(new_v / (1.0 - beta_two**20)) + epsilon)
        looped(HALF, 16, adam)
    for i, (src, dst) in enumerate(((mbuf, new_first), (vbuf, new_second))):
        store = pltpu.make_async_copy(src, dst, lsem.at[i])
        store.start()
        stores.append(store)

    rpart[...] = jnp.dot(dbuf[...], skbuf[...], precision=hp, preferred_element_type=f32)
    parts = []
    for k in range(1, 8):
        where, other = roller(k)
        parts.append(send(rpart.at[pl.ds(pl.multiple_of(other * PIECE, 8), PIECE)], rrecv.at[k - 1], where))
    my_piece = pl.ds(pl.multiple_of(r * PIECE, 8), PIECE)
    total = rpart[my_piece]
    for k in range(7):
        parts[k].wait_recv()
        total = total + rrecv[k]
    rfull[my_piece] = total
    parts = [send(rfull.at[my_piece], rfull.at[my_piece], roller(k)[0]) for k in range(1, 8)]
    for part in parts:
        part.wait_recv()

    gpart[...] = lax.dot_general(rfull[...], rfull[...], DN0, precision=hp, preferred_element_type=f32)
    my_half = pl.ds(pl.multiple_of(c * 64, 64), 64)
    other_half = pl.ds(pl.multiple_of((1 - c) * 64, 64), 64)
    copy = send(gpart.at[other_half], gcrecv, sibling)
    spart[...] = lax.dot_general(rfull[...], dbuf[...], DN0, precision=hp, preferred_element_type=f32)
    scopy = send(spart.at[other_half], screcv, sibling)
    copy.wait_recv()
    gslots[q] = gpart[my_half] + gcrecv[...]
    parts = [send(gslots.at[q], gslots.at[q], chip(k)[0]) for k in range(1, 8)]

    scopy.wait_recv()
    spart[my_half] = spart[my_half] + screcv[...]
    sparts = []
    for k in range(1, 8):
        where, other = chip(k)
        sparts.append(send(spart.at[pl.ds(pl.multiple_of(c * 64 + other * 8, 8), 8)], sslots.at[q], where))
    sslots[q] = spart[pl.ds(pl.multiple_of(c * 64 + q * 8, 8), 8)]

    for part in parts:
        part.wait_recv()
    total = gslots[0]
    for k in range(1, 8):
        total = total + gslots[k]
    ghalf[c] = total
    copy = send(ghalf.at[c], ghalf.at[c], sibling)

    for part in sparts:
        part.wait_recv()
    total = sslots[0]
    for k in range(1, 8):
        total = total + sslots[k]
    s, t = c * y + (1 - c) * z, c * z + (1 - c) * y
    row = pl.ds(pl.multiple_of(xh * 8, 8), 8)
    s_out[c, s, t, xl, row] = total
    parts = [
        send(s_out.at[c, s, t, xl, row], s_out.at[c, s, t, xl, row], around_x(k)) for k in range(1, 4)
    ]

    @pl.when((y == z) & (xh == xl))
    def _():
        r_out[c] = rfull[...]
    rcopies = []
    for k in range(1, 8):
        rcopies.append(remote(r_out.at[c], r_out.at[c], chip(k)[0]))

    @pl.when((y == z) & (xh == xl))
    def _():
        for rcopy in rcopies:
            rcopy.start()

    for part in parts:
        part.wait_recv()

    def along_t(k):
        return dev(y=(y + (1 - c) * k) % 4, z=(z + c * k) % 4)

    def along_s(k):
        return dev(y=(y + c * k) % 4, z=(z + (1 - c) * k) % 4)
    parts = [send(s_out.at[c, s, t], s_out.at[c, s, t], along_t(k)) for k in (1, 3, 2)]
    for part in parts:
        part.wait_recv()
    parts = [send(s_out.at[c, s], s_out.at[c, s], along_s(k)) for k in (1, 3, 2)]

    copy.wait_recv()
    gram_out[0:64] = ghalf[0]
    gram_out[64:128] = ghalf[1]
    for k in range(1, 8):
        @pl.when((z * 2 + xl + k) % 8 == q)
        def _():
            rcopies[k - 1].wait_recv()
    rcopy = send(r_out.at[c], r_out.at[c], sibling)

    copies = [send(s_out.at[c, s], s_out.at[c, s], sibling)]
    for k, part in zip((1, 3, 2), parts):
        part.wait_recv()
        have = (s + 4 - k) % 4
        copies.append(send(s_out.at[c, have], s_out.at[c, have], sibling))
    rcopy.wait_recv()
    for part in copies:
        part.wait_recv()

    for part in pending:
        part.wait_send()

    @pl.when((y == z) & (xh == xl))
    def _():
        for part in rcopies:
            part.wait_send()
    for store in stores:
        store.wait()


def local(activations, cotangent, first_moment, second_moment, sketch):
    any_spec, vmem = pl.BlockSpec(memory_space=pl.ANY), pl.BlockSpec(memory_space=pltpu.VMEM)
    state = jax.ShapeDtypeStruct((ROWS, COLS), f32)
    new_first, new_second, gram, s_all, r_all = pl.pallas_call(
        kernel,
        name="step",
        out_shape=(
            state, state,
            jax.ShapeDtypeStruct((RANK, RANK), f32),
            jax.ShapeDtypeStruct((2, 4, 4, 2, 16, COLS), f32),
            jax.ShapeDtypeStruct((2, ROWS, RANK), f32),
        ),
        in_specs=[any_spec] * 5,
        out_specs=(any_spec, any_spec, vmem, vmem, vmem),
        scratch_shapes=[
            pltpu.VMEM((8, TOK, 640), bf16),
            pltpu.VMEM((TOK, COLS), bf16),
            pltpu.VMEM((640, COLS), f32),
            pltpu.VMEM((8, ROWS, COLS), f32),
            pltpu.VMEM((8, ROWS, COLS), bf16),
            pltpu.VMEM((8, ROWS, COLS), bf16),
            pltpu.VMEM((6, ROWS, COLS), bf16),
            pltpu.VMEM((2, 2, HALF, COLS), bf16),
            pltpu.VMEM((2, 2, ROWS, COLS), bf16),
            pltpu.VMEM((ROWS, COLS), bf16),
            pltpu.VMEM((ROWS, COLS), bf16),
            pltpu.VMEM((ROWS, COLS), f32),
            pltpu.VMEM((ROWS, COLS), f32),
            pltpu.VMEM((ROWS, COLS), f32),
            pltpu.VMEM((COLS, RANK), f32),
            pltpu.VMEM((ROWS, RANK), f32),
            pltpu.VMEM((7, PIECE, RANK), f32),
            pltpu.VMEM((ROWS, RANK), f32),
            pltpu.VMEM((RANK, RANK), f32),
            pltpu.VMEM((64, RANK), f32),
            pltpu.VMEM((8, 64, RANK), f32),
            pltpu.VMEM((2, 64, RANK), f32),
            pltpu.VMEM((RANK, COLS), f32),
            pltpu.VMEM((64, COLS), f32),
            pltpu.VMEM((8, 8, COLS), f32),
            pltpu.SemaphoreType.DMA((12,)),
            pltpu.SemaphoreType.DMA((SEMS,)),
            pltpu.SemaphoreType.DMA((SEMS,)),
        ],
        compiler_params=pltpu.CompilerParams(
            collective_id=0, has_side_effects=True, vmem_limit_bytes=58 << 20),
    )(activations, cotangent, first_moment, second_moment, sketch)
    lower = jnp.linalg.cholesky(gram)
    inverse = lax.linalg.triangular_solve(lower, jnp.eye(RANK, dtype=f32), left_side=True, lower=True)
    low = s_all[0].transpose(1, 3, 0, 2, 4)
    high = s_all[1].transpose(0, 3, 1, 2, 4)
    s_full = jnp.stack([low, high]).reshape(RANK, D)
    coeffs = jnp.dot(inverse, s_full, precision=hp).astype(bf16)
    basis = lax.dot_general(r_all.reshape(2 * ROWS, RANK), inverse, (((1,), (1,)), ((), ())), precision=hp).astype(bf16)
    rebuilt = jnp.dot(basis, coeffs, preferred_element_type=f32).astype(bf16)
    return new_first, new_second, rebuilt


def solution(mesh):
    placed = (P("fsdp", None), P("fsdp", "roll"), P("fsdp", "roll"), P("fsdp", "roll"), P("roll", None))
    return jax.shard_map(
        local,
        mesh=mesh,
        in_specs=placed,
        out_specs=(P("fsdp", "roll"), P("fsdp", "roll"), P("roll", None)),
        check_vma=False,
    )
```

time: 554 us -> 141 us (0.25)
  the two profiles are of different devices: /device:TPU:1 before, /device:TPU:5 now
where the time goes in v1:
time: 141 us; the launch traced here: 140 us
  Pallas kernels  96.5 us (68%)
  other arithmetic  23.9 us (17%)
  local copies, waits for them, and re-layouts  10.7 us (8%)
  matrix products  8.65 us (6%)
    pallas_call x1, Pallas kernels, local(): pl.pallas_call(kernel, name='step', out_shape=(state, state, jax.ShapeDty...  96.5 us
    another operation x3, other arithmetic, local(): lower = jnp.linalg.cholesky(gram)  12.4 us
    another operation x2, other arithmetic, local(): lax.linalg.triangular_solve(lower, jnp.eye(RANK, dtype=f32), left_side=Tr...  10.5 us
    dot_general x1, matrix products, local(): rebuilt = jnp.dot(basis, coeffs, preferred_element_type=f32).astype(bf16)  4.65 us
    another operation x3, local copies, waits for them, and re-layouts, local(): s_full = jnp.stack([low, high]).reshape(RANK, D)  4.36 us
    reshape x1, local copies, waits for them, and re-layouts, local(): s_full = jnp.stack([low, high]).reshape(RANK, D)  3.45 us

profile of v1, /device:TPU:5, one launch (start us, length us, event | category | flops | bytes accessed | tf_op | source)
XLA Modules:
  0.0 140.4 jit_solution(14569996607206386929)
XLA Ops:
  0.6 96.5 %step.1 = (f32[320,640]{1,0:T(8,128)}, f32[320,640]{1,0:T(8,128)}, f32[128,128]{1,0:T(8,128)}, f32[2,4,4,2,16,640]{5,4,3,2,1,0:T(8,128)}, f32[2,320,128]{2,1,0:T(8,128)}) custom-call(bf16[1024,5120]{1,0:T(8,128)(2,1)} %act.1, bf16[1024,640]{1,0:T(8,128)(2,1)} %cot.1, f32[320,640]{1,0:T(8,128)} %first.1, f32[320,640]{1,0:T(8,128)} %second.1, f32[640,128]{1,0:T(8,128)} %sketch.1), custom_call_target="tpu_custom_call" | custom-call | tf_op jit(solution)/shard_map/step/pallas_call | solution.py:322
  97.1 0.0 copy-start
  97.1 1.1 copy.10
  98.2 0.9 fusion.3
  99.1 11.7 %cholesky.17 = f32[128,128]{1,0:T(8,128)S(1)} custom-call(f32[128,128]{1,0:T(8,128)S(1)} %fusion.3), custom_call_target="Cholesky" | custom-call | tf_op jit(solution)/shard_map/jit(cholesky)/cholesky | solution.py:366
  110.8 0.6 compare_reduce_fusion
  111.5 0.7 fusion
  112.1 9.8 %custom-call.6 = f32[1,128,128]{1,2,0:T(8,128)S(1)} custom-call(f32[1,128,128]{2,1,0:T(8,128)S(1)} %fusion), custom_call_target="InvertDiagBlocksLowerTriangular" | custom-call | tf_op jit(solution)/shard_map/triangular_solve | solution.py:367
  121.9 0.2 fusion.1
  122.2 1.4 convolution_convert_fusion.2
  123.6 1.4 %slice_bitcast_fusion.1 = f32[1,4,16,4,2,640]{5,2,4,3,1,0:T(8,128)S(1)} fusion(f32[2,4,4,2,16,640]{5,4,3,2,1,0:T(8,128)} %get-tuple-element.12), kind=kLoop, calls=%fused_computation.4 | loop fusion | bytes 2621440 | tf_op jit(solution)/shard_map/stack | solution.py:370
  125.0 0.0 copy-done
  125.0 0.1 slice_bitcast_fusion
  125.2 0.2 pad_maximum_fusion
  125.3 2.8 %copy.12 = f32[2,4,16,4,2,640]{5,4,3,2,1,0:T(2,128)} copy(f32[2,4,16,4,2,640]{5,2,4,3,1,0:T(8,128)S(1)} %pad_maximum_fusion) | data formatting | bytes 5242880 | tf_op jit(solution)/shard_map/stack | solution.py:370
  128.2 3.5 %reshape.22 = f32[128,5120]{1,0:T(8,128)S(1)} reshape(f32[2,4,16,4,2,640]{5,4,3,2,1,0:T(2,128)} %copy.12) | data formatting | bytes 5242880 | tf_op jit(solution)/shard_map/reshape | solution.py:370
  131.6 2.3 %convolution_convert_fusion.1 = bf16[128,5120]{1,0:T(8,128)(2,1)S(1)} fusion(f32[128,128]{1,0:T(8,128)S(1)} %fusion.1, f32[128,5120]{1,0:T(8,128)S(1)} %reshape.22), kind=kOutput, calls=%fused_computation.1 | convolution fusion | flops 1007288320 | bytes 3997696 | tf_op jit(solution)/shard_map/dot_general | solution.py:371
  134.0 0.0 copy-start.2
  134.0 0.0 copy-start.1
  134.0 4.6 %convolution_convert_fusion = bf16[640,5120]{1,0:T(8,128)(2,1)} fusion(bf16[640,128]{1,0:T(8,128)(2,1)S(1)} %convolution_convert_fusion.2, bf16[128,5120]{1,0:T(8,128)(2,1)S(1)} %convolution_convert_fusion.1), kind=kOutput, calls=%fused_computation | convolution fusion | flops 842137600 | bytes 8028160 | tf_op jit(solution)/shard_map/dot_general | solution.py:373
  138.6 0.0 copy-done.2
  138.7 0.9 copy.17
  139.5 0.0 copy-done.1
  139.5 0.9 copy.18
  (1 shorter events, 0.0 us)
Async XLA Ops:
  97.1 27.9 %copy-start = (f32[2,4,4,2,16,640]{5,4,3,2,1,0:T(8,128)S(1)}, f32[2,4,4,2,16,640]{5,4,3,2,1,0:T(8,128)}, u32[]{:S(2)}) copy-start(f32[2,4,4,2,16,640]{5,4,3,2,1,0:T(8,128)} %get-tuple-element.12) | copy-start | bytes 7864324
  134.0 4.7 %copy-start.2 = (f32[320,640]{1,0:T(8,128)S(1)}, f32[320,640]{1,0:T(8,128)}, u32[]{:S(2)}) copy-start(f32[320,640]{1,0:T(8,128)} %get-tuple-element.16) | copy-start | bytes 2457604
  134.0 5.6 %copy-start.1 = (f32[320,640]{1,0:T(8,128)S(1)}, f32[320,640]{1,0:T(8,128)}, u32[]{:S(2)}) copy-start(f32[320,640]{1,0:T(8,128)} %get-tuple-element.17) | copy-start | bytes 2457604

commit v2 on v1

--- a/solution.py
+++ b/solution.py
@@ -14,6 +14,7 @@
 MESH = pl.DeviceIdType.MESH
 f32, bf16 = jnp.float32, jnp.bfloat16
 DN0 = (((0,), (0,)), ((), ()))
+DN1 = (((1,), (1,)), ((), ()))
 
 D, TOK, RANK = 5120, 1024, 128
 COLS = 640
@@ -32,12 +33,54 @@
     lax.fori_loop(0, total // step, one, 0)
 
 
+def split3(v):
+    a = v.astype(bf16).astype(f32); v = v - a
+    b = v.astype(bf16).astype(f32)
+    return a, b, (v - b).astype(bf16).astype(f32)
+
+def factor_inverse(gram_ref, inv_ref):
+    lane = lax.broadcasted_iota(jnp.int32, (8, 128), 1)
+    sub = lax.broadcasted_iota(jnp.int32, (8, 128), 0)
+    panels = [gram_ref[8 * i:8 * i + 8, :] for i in range(16)]
+    for k in range(16):
+        panel = panels[k]
+        scale = jnp.zeros((8, 128), f32)
+        for j in range(8):
+            p = 8 * k + j
+            col = jnp.broadcast_to(panel[:, p:p + 1], (8, 128))
+            pivot = jnp.broadcast_to(col[j:j + 1, :], (8, 128))
+            recip = 1.0 / pivot
+            scale = jnp.where(sub == j, recip, scale)
+            m = jnp.where(sub > j, -col * recip, 0.0)
+            row = jnp.broadcast_to(jnp.where(lane[j:j + 1] == p, 1.0, panel[j:j + 1, :]), (8, 128))
+            panel = jnp.where((lane == p) & (sub > j), 0.0, panel) + m * row
+        panels[k] = panel
+        if k < 15:
+            inside = (lane >= 8 * k) & (lane < 8 * k + 8)
+            ext = jnp.where(inside & (lane - 8 * k > sub), 0.0, panel)
+            ext = jnp.where(inside & (lane - 8 * k == sub), 1.0, ext)
+            lhs = -panel * scale
+            a1, a2, a3 = split3(lhs)
+            b1, b2, b3 = split3(ext)
+            left = jnp.concatenate([a1, a1, a2, a2, a1, a3], axis=0).astype(bf16)
+            right = jnp.concatenate([b1, b2, b1, b2, b3, b1], axis=0).astype(bf16)
+            upd = lax.dot_general(left, right, DN0, preferred_element_type=f32)
+            for i in range(k + 1, 16):
+                panels[i] = jnp.where(inside, 0.0, panels[i]) + upd[8 * i:8 * i + 8, :]
+        yield k
+    for k in range(16):
+        at = lane == sub + 8 * k
+        d = jnp.sum(jnp.where(at, panels[k], 0.0), axis=1, keepdims=True)
+        m = jnp.where(lane < sub + 8 * k, panels[k], jnp.where(at, 1.0, 0.0))
+        inv_ref[8 * k:8 * k + 8, :] = m * lax.rsqrt(d)
+
+
 def kernel(
     act, cot, first, second, sketch,
-    new_first, new_second, gram_out, s_out, r_out,
+    new_first, new_second, coeffs_out, basis_out,
     abuf, cbuf, pbuf, own, psend, crecv, ysend, y1recv, y2recv, xsend, xrecv,
-    mbuf, vbuf, dbuf, skbuf, rpart, rrecv, rfull, gpart, gcrecv, gslots, ghalf,
-    spart, screcv, sslots,
+    mbuf, vbuf, dbuf, skbuf, rpart, rrecv, rfull, r_out, gpart, gcrecv, gslots, gfull,
+    spart, screcv, sslots, s_out, inverse,
     lsem, ssem, rsem,
 ):
     f, r = lax.axis_index("fsdp"), lax.axis_index("roll")
@@ -221,115 +264,155 @@
         total = total + rrecv[k]
     rfull[my_piece] = total
     parts = [send(rfull.at[my_piece], rfull.at[my_piece], roller(k)[0]) for k in range(1, 8)]
+    swap = remote(rfull.at[my_piece], r_out.at[c, my_piece], dev(y=z, xh=xl, z=y, xl=xh))
+    own_piece = pl.ds(pl.multiple_of(q * PIECE, 8), PIECE)
+    swapped = (y != z) | (xh != xl)
+
+    @pl.when(swapped)
+    def _():
+        swap.start()
+
+    @pl.when(jnp.logical_not(swapped))
+    def _():
+        r_out[c, own_piece] = rfull[my_piece]
     for part in parts:
         part.wait_recv()
 
-    gpart[...] = lax.dot_general(rfull[...], rfull[...], DN0, precision=hp, preferred_element_type=f32)
     my_half = pl.ds(pl.multiple_of(c * 64, 64), 64)
     other_half = pl.ds(pl.multiple_of((1 - c) * 64, 64), 64)
-    copy = send(gpart.at[other_half], gcrecv, sibling)
+    my_rows = pl.ds(pl.multiple_of(c * 64 + q * 8, 8), 8)
+    gpart[...] = lax.dot_general(rfull[...], rfull[...], DN0, precision=hp, preferred_element_type=f32)
+    gcopy = send(gpart.at[other_half], gcrecv, sibling)
     spart[...] = lax.dot_general(rfull[...], dbuf[...], DN0, precision=hp, preferred_element_type=f32)
     scopy = send(spart.at[other_half], screcv, sibling)
-    copy.wait_recv()
-    gslots[q] = gpart[my_half] + gcrecv[...]
-    parts = [send(gslots.at[q], gslots.at[q], chip(k)[0]) for k in range(1, 8)]
-
+
+    def scatter(mine, slots):
+        sent = []
+        for k in range(1, 8):
+            where, other = chip(k)
+            sent.append(send(mine.at[pl.ds(pl.multiple_of(c * 64 + other * 8, 8), 8)], slots.at[q], where))
+        slots[q] = mine[my_rows]
+        return sent
+
+    def gathered(sent, slots):
+        for part in sent:
+            part.wait_recv()
+        total = slots[0]
+        for k in range(1, 8):
+            total = total + slots[k]
+        return total
+
+    gcopy.wait_recv()
+    gpart[my_half] = gpart[my_half] + gcrecv[...]
+    gsent = scatter(gpart, gslots)
     scopy.wait_recv()
     spart[my_half] = spart[my_half] + screcv[...]
-    sparts = []
-    for k in range(1, 8):
-        where, other = chip(k)
-        sparts.append(send(spart.at[pl.ds(pl.multiple_of(c * 64 + other * 8, 8), 8)], sslots.at[q], where))
-    sslots[q] = spart[pl.ds(pl.multiple_of(c * 64 + q * 8, 8), 8)]
-
-    for part in parts:
-        part.wait_recv()
-    total = gslots[0]
-    for k in range(1, 8):
-        total = total + gslots[k]
-    ghalf[c] = total
-    copy = send(ghalf.at[c], ghalf.at[c], sibling)
-
-    for part in sparts:
-        part.wait_recv()
-    total = sslots[0]
-    for k in range(1, 8):
-        total = total + sslots[k]
+    ssent = scatter(spart, sslots)
+    gfull[my_rows] = gathered(gsent, gslots)
+    gsent = [send(gfull.at[my_rows], gfull.at[my_rows], chip(k)[0]) for k in range(1, 8)]
+
+    @pl.when(swapped)
+    def _():
+        swap.wait_recv()
+    rsent = [send(r_out.at[c, own_piece], r_out.at[c, own_piece], chip(k)[0]) for k in range(1, 8)]
+
     s, t = c * y + (1 - c) * z, c * z + (1 - c) * y
     row = pl.ds(pl.multiple_of(xh * 8, 8), 8)
-    s_out[c, s, t, xl, row] = total
-    parts = [
-        send(s_out.at[c, s, t, xl, row], s_out.at[c, s, t, xl, row], around_x(k)) for k in range(1, 4)
-    ]
-
-    @pl.when((y == z) & (xh == xl))
-    def _():
-        r_out[c] = rfull[...]
-    rcopies = []
-    for k in range(1, 8):
-        rcopies.append(remote(r_out.at[c], r_out.at[c], chip(k)[0]))
-
-    @pl.when((y == z) & (xh == xl))
-    def _():
-        for rcopy in rcopies:
-            rcopy.start()
-
-    for part in parts:
-        part.wait_recv()
+    s_out[c, s, t, xl, row] = gathered(ssent, sslots)
+    ssent = [send(s_out.at[c, s, t, xl, row], s_out.at[c, s, t, xl, row], around_x(k)) for k in range(1, 4)]
+    for part in gsent:
+        part.wait_recv()
+    gcopy = send(gfull.at[my_half], gfull.at[my_half], sibling)
 
     def along_t(k):
         return dev(y=(y + (1 - c) * k) % 4, z=(z + c * k) % 4)
 
     def along_s(k):
         return dev(y=(y + c * k) % 4, z=(z + (1 - c) * k) % 4)
-    parts = [send(s_out.at[c, s, t], s_out.at[c, s, t], along_t(k)) for k in (1, 3, 2)]
-    for part in parts:
-        part.wait_recv()
-    parts = [send(s_out.at[c, s], s_out.at[c, s], along_s(k)) for k in (1, 3, 2)]
-
-    copy.wait_recv()
-    gram_out[0:64] = ghalf[0]
-    gram_out[64:128] = ghalf[1]
-    for k in range(1, 8):
-        @pl.when((z * 2 + xl + k) % 8 == q)
-        def _():
-            rcopies[k - 1].wait_recv()
+
+    gcopy.wait_recv()
+    steps = factor_inverse(gfull, inverse)
+    next(steps)
+    for part in ssent:
+        part.wait_recv()
+    ssent = [send(s_out.at[c, s, t], s_out.at[c, s, t], along_t(k)) for k in (1, 3, 2)]
+    for _ in range(4):
+        next(steps)
+    for part in ssent:
+        part.wait_recv()
+    ssent = [send(s_out.at[c, s], s_out.at[c, s], along_s(k)) for k in (1, 3, 2)]
+    copies = [send(s_out.at[c, s], s_out.at[c, s], sibling)]
+    for _ in range(2):
+        next(steps)
+    for part in rsent:
+        part.wait_recv()
     rcopy = send(r_out.at[c], r_out.at[c], sibling)
-
-    copies = [send(s_out.at[c, s], s_out.at[c, s], sibling)]
-    for k, part in zip((1, 3, 2), parts):
+    for k, part in zip((1, 3, 2), ssent):
+        for _ in range(3):
+            next(steps)
         part.wait_recv()
         have = (s + 4 - k) % 4
         copies.append(send(s_out.at[c, have], s_out.at[c, have], sibling))
+    for _ in steps:
+        pass
     rcopy.wait_recv()
+    for core in range(2):
+        basis_out[core * ROWS:(core + 1) * ROWS] = lax.dot_general(
+            r_out[core], inverse[...], DN1, precision=hp, preferred_element_type=f32).astype(bf16)
     for part in copies:
         part.wait_recv()
+
+    def block(i, carry):
+        bz, bxl = i // 2, i % 2
+        rows = [s_out[0, bz, by, bxl] for by in range(4)] + [s_out[1, by, bz, bxl] for by in range(4)]
+        coeffs_out[:, pl.ds(pl.multiple_of(i * COLS, COLS), COLS)] = jnp.dot(
+            inverse[...], jnp.concatenate(rows, axis=0), precision=hp, preferred_element_type=f32).astype(bf16)
+        return carry
+    lax.fori_loop(0, 8, block, 0)
 
     for part in pending:
         part.wait_send()
 
-    @pl.when((y == z) & (xh == xl))
+    @pl.when(swapped)
     def _():
-        for part in rcopies:
-            part.wait_send()
+        swap.wait_send()
     for store in stores:
         store.wait()
 
 
+def rebuild(basis, coeffs, first, second, rebuilt, new_first, new_second, bbuf, cbuf, obuf, sem):
+    copies = [pltpu.make_async_copy(basis, bbuf, sem.at[2])]
+    copies += [pltpu.make_async_copy(coeffs.at[:, pl.ds(i * 1280, 1280)], cbuf.at[i], sem.at[3 + i]) for i in range(4)]
+    kept = [pltpu.make_async_copy(first, new_first, sem.at[0]), pltpu.make_async_copy(second, new_second, sem.at[1])]
+    for copy in copies + kept:
+        copy.start()
+    copies[0].wait()
+    for i in range(4):
+        copies[1 + i].wait()
+        columns = pl.ds(i * 1280, 1280)
+        for j in range(2):
+            rows = pl.ds(j * ROWS, ROWS)
+            obuf[i, rows] = jnp.dot(bbuf[rows], cbuf[i], preferred_element_type=f32).astype(bf16)
+            copy = pltpu.make_async_copy(obuf.at[i, rows], rebuilt.at[rows, columns], sem.at[7 + 2 * i + j])
+            copy.start()
+            kept.append(copy)
+    for copy in kept:
+        copy.wait()
+
+
 def local(activations, cotangent, first_moment, second_moment, sketch):
-    any_spec, vmem = pl.BlockSpec(memory_space=pl.ANY), pl.BlockSpec(memory_space=pltpu.VMEM)
+    hbm, vmem = pl.BlockSpec(memory_space=pltpu.HBM), pl.BlockSpec(memory_space=pltpu.VMEM)
     state = jax.ShapeDtypeStruct((ROWS, COLS), f32)
-    new_first, new_second, gram, s_all, r_all = pl.pallas_call(
+    first, second, coeffs, basis = pl.pallas_call(
         kernel,
         name="step",
         out_shape=(
             state, state,
-            jax.ShapeDtypeStruct((RANK, RANK), f32),
-            jax.ShapeDtypeStruct((2, 4, 4, 2, 16, COLS), f32),
-            jax.ShapeDtypeStruct((2, ROWS, RANK), f32),
+            jax.ShapeDtypeStruct((RANK, D), bf16),
+            jax.ShapeDtypeStruct((2 * ROWS, RANK), bf16),
         ),
-        in_specs=[any_spec] * 5,
-        out_specs=(any_spec, any_spec, vmem, vmem, vmem),
+        in_specs=[hbm] * 5,
+        out_specs=(hbm, hbm, vmem, vmem),
         scratch_shapes=[
             pltpu.VMEM((8, TOK, 640), bf16),
             pltpu.VMEM((TOK, COLS), bf16),
@@ -349,13 +432,16 @@
             pltpu.VMEM((ROWS, RANK), f32),
             pltpu.VMEM((7, PIECE, RANK), f32),
             pltpu.VMEM((ROWS, RANK), f32),
+            pltpu.VMEM((2, ROWS, RANK), f32),
             pltpu.VMEM((RANK, RANK), f32),
             pltpu.VMEM((64, RANK), f32),
-            pltpu.VMEM((8, 64, RANK), f32),
-            pltpu.VMEM((2, 64, RANK), f32),
+            pltpu.VMEM((8, 8, RANK), f32),
+            pltpu.VMEM((RANK, RANK), f32),
             pltpu.VMEM((RANK, COLS), f32),
             pltpu.VMEM((64, COLS), f32),
             pltpu.VMEM((8, 8, COLS), f32),
+            pltpu.VMEM((2, 4, 4, 2, 16, COLS), f32),
+            pltpu.VMEM((RANK, RANK), f32),
             pltpu.SemaphoreType.DMA((12,)),
             pltpu.SemaphoreType.DMA((SEMS,)),
             pltpu.SemaphoreType.DMA((SEMS,)),
@@ -363,14 +449,20 @@
         compiler_params=pltpu.CompilerParams(
             collective_id=0, has_side_effects=True, vmem_limit_bytes=58 << 20),
     )(activations, cotangent, first_moment, second_moment, sketch)
-    lower = jnp.linalg.cholesky(gram)
-    inverse = lax.linalg.triangular_solve(lower, jnp.eye(RANK, dtype=f32), left_side=True, lower=True)
-    low = s_all[0].transpose(1, 3, 0, 2, 4)
-    high = s_all[1].transpose(0, 3, 1, 2, 4)
-    s_full = jnp.stack([low, high]).reshape(RANK, D)
-    coeffs = jnp.dot(inverse, s_full, precision=hp).astype(bf16)
-    basis = lax.dot_general(r_all.reshape(2 * ROWS, RANK), inverse, (((1,), (1,)), ((), ())), precision=hp).astype(bf16)
-    rebuilt = jnp.dot(basis, coeffs, preferred_element_type=f32).astype(bf16)
+    rebuilt, new_first, new_second = pl.pallas_call(
+        rebuild,
+        name="rebuild",
+        out_shape=(jax.ShapeDtypeStruct((COLS, D), bf16), state, state),
+        in_specs=[hbm] * 4,
+        out_specs=(hbm,) * 3,
+        scratch_shapes=[
+            pltpu.VMEM((2 * ROWS, RANK), bf16),
+            pltpu.VMEM((4, RANK, 1280), bf16),
+            pltpu.VMEM((4, COLS, 1280), bf16),
+            pltpu.SemaphoreType.DMA((15,)),
+        ],
+        compiler_params=pltpu.CompilerParams(vmem_limit_bytes=60 << 20),
+    )(basis, coeffs, first, second)
     return new_first, new_second, rebuilt
 
 

time: 141 us -> 157 us (1.11)
  the two profiles are of different devices: /device:TPU:5 before, /device:TPU:1 now
where the time goes in v2:
time: 157 us
  Pallas kernels  156 us (99%)
    pallas_call x1, Pallas kernels, local(): pl.pallas_call(kernel, name='step', out_shape=(state, state, jax.ShapeDty...  105 us
    pallas_call x1, Pallas kernels, local(): pl.pallas_call(rebuild, name='rebuild', out_shape=(jax.ShapeDtypeStruct((...  50.9 us

profile of v2, /device:TPU:1, one launch (start us, length us, event | category | flops | bytes accessed | tf_op | source)
XLA Modules:
  0.0 156.7 jit_solution(3471537963665863656)
XLA Ops:
  0.6 105.0 %step.1 = (f32[320,640]{1,0:T(8,128)}, f32[320,640]{1,0:T(8,128)}, bf16[128,5120]{1,0:T(8,128)(2,1)}, bf16[640,128]{1,0:T(8,128)(2,1)}) custom-call(bf16[1024,5120]{1,0:T(8,128)(2,1)} %act.1, bf16[1024,640]{1,0:T(8,128)(2,1)} %cot.1, f32[320,640]{1,0:T(8,128)} %first.1, f32[320,640]{1,0:T(8,128)} %second.1, f32[640,128]{1,0:T(8,128)} %sketch.1), custom_call_target="tpu_custom_call" | custom-call | tf_op jit(solution)/shard_map/step/pallas_call | solution.py:406
  105.6 50.9 %rebuild.1 = (bf16[640,5120]{1,0:T(8,128)(2,1)}, f32[320,640]{1,0:T(8,128)}, f32[320,640]{1,0:T(8,128)}) custom-call(bf16[640,128]{1,0:T(8,128)(2,1)} %get-tuple-element.10.basis, bf16[128,5120]{1,0:T(8,128)(2,1)} %get-tuple-element.11.coeffs, f32[320,640]{1,0:T(8,128)} %get-tuple-element.12.first, f32[320,640]{1,0:T(8,128)} %get-tuple-element.13.second), custom_call_target="tpu_custom_call" | custom-call | tf_op jit(solution)/shard_map/rebuild/pallas_call | solution.py:452

commit v3 on v2

--- a/solution.py
+++ b/solution.py
@@ -19,11 +19,13 @@
 D, TOK, RANK = 5120, 1024, 128
 COLS = 640
 ROWS = 320
-HALF = 160
+XROWS = 128
+XHALF = XROWS // 2
+HALF = (ROWS - XROWS) // 2
 PIECE = ROWS // 8
 
 ORDER = ((2, 1), (2, 0), (1, 1), (3, 1), (1, 0), (3, 0), (0, 1), (0, 0))
-SEMS = 96
+SEMS = 112
 
 
 def looped(total, step, body):
@@ -78,7 +80,7 @@
 def kernel(
     act, cot, first, second, sketch,
     new_first, new_second, coeffs_out, basis_out,
-    abuf, cbuf, pbuf, own, psend, crecv, ysend, y1recv, y2recv, xsend, xrecv,
+    abuf, cbuf, pbuf, own, psend, crecv, ysend, y1recv, y1x, y2recv, xfsend, xfrecv, xsend, xrecv,
     mbuf, vbuf, dbuf, skbuf, rpart, rrecv, rfull, r_out, gpart, gcrecv, gslots, gfull,
     spart, screcv, sslots, s_out, inverse,
     lsem, ssem, rsem,
@@ -165,88 +167,131 @@
             pl.semaphore_wait(barrier, len(greeted))
         halves.append(send(psend.at[k], crecv.at[k], sibling))
 
-    step_one, step_two = {}, {}
+    step_one, step_two, first_x, one_x, two_x = {}, {}, {}, {}, {}
+    ways = (plus, minus)
+
+    def summed(k, at):
+        return own[k, at] + crecv[k, at].astype(f32)
 
     def post(k):
         dy, dxh = ORDER[k]
         halves[k].wait_recv()
+        if dxh == 1:
+            def add(o):
+                xfsend[dy, pl.ds(o, 32)] = summed(k, pl.ds(o, 32)).astype(bf16)
+            looped(XROWS, 32, add)
+            first_x[dy] = send(xfsend.at[dy], xfrecv.at[dy], across)
         if dy == 2:
             def add(o):
-                ysend[k, pl.ds(o, 32)] = (own[k, pl.ds(o, 32)] + crecv[k, pl.ds(o, 32)].astype(f32)).astype(bf16)
-            looped(ROWS, 32, add)
-            for way, where in enumerate((plus, minus)):
+                at = pl.ds(XROWS + o, 32)
+                ysend[k, at] = summed(k, at).astype(bf16)
+            looped(ROWS - XROWS, 32, add)
+            for way, where in enumerate(ways):
                 step_one[way, dxh] = send(
-                    ysend.at[k, pl.ds(way * HALF, HALF)], y1recv.at[way, dxh], where)
-        elif dy == 0:
+                    ysend.at[k, pl.ds(XROWS + way * HALF, HALF)], y1recv.at[way, dxh], where)
+        elif dy != 0:
+            way = 0 if dy == 1 else 1
+            alone = XROWS + (1 - way) * HALF
+
             def add(o):
-                own[k, pl.ds(o, 32)] = own[k, pl.ds(o, 32)] + crecv[k, pl.ds(o, 32)].astype(f32)
-            looped(ROWS, 32, add)
-        else:
-            way = 0 if dy == 1 else 1
-            alone = (1 - way) * HALF
-
-            def add(o):
-                ysend[k, pl.ds(alone + o, 32)] = (
-                    own[k, pl.ds(alone + o, 32)] + crecv[k, pl.ds(alone + o, 32)].astype(f32)).astype(bf16)
+                at = pl.ds(alone + o, 32)
+                ysend[k, at] = summed(k, at).astype(bf16)
             looped(HALF, 32, add)
             step_two[way, dxh, 1] = send(
-                ysend.at[k, pl.ds(alone, HALF)], y2recv.at[way, dxh, pl.ds(alone, HALF)],
-                plus if way == 0 else minus)
+                ysend.at[k, pl.ds(alone, HALF)], y2recv.at[way, dxh, pl.ds(alone, HALF)], ways[way])
 
     def accumulate(dxh):
         for way, dy in ((0, 1), (1, 3)):
             k = ORDER.index((dy, dxh))
             step_one[way, dxh].wait_recv()
-            start = way * HALF
+            start = XROWS + way * HALF
 
             def add(o):
-                ysend[k, pl.ds(start + o, 32)] = (
-                    own[k, pl.ds(start + o, 32)] + crecv[k, pl.ds(start + o, 32)].astype(f32)
-                    + y1recv[way, dxh, pl.ds(o, 32)].astype(f32)).astype(bf16)
+                at = pl.ds(start + o, 32)
+                ysend[k, at] = (summed(k, at) + y1recv[way, dxh, pl.ds(o, 32)].astype(f32)).astype(bf16)
             looped(HALF, 32, add)
             step_two[way, dxh, 0] = send(
-                ysend.at[k, pl.ds(start, HALF)], y2recv.at[way, dxh, pl.ds(start, HALF)],
-                plus if way == 0 else minus)
+                ysend.at[k, pl.ds(start, HALF)], y2recv.at[way, dxh, pl.ds(start, HALF)], ways[way])
+
+    def crossed(dy):
+        k = ORDER.index((dy, 0))
+        first_x[dy].wait_recv()
+        start, size = {2: (0, XROWS), 1: (XHALF, XHALF), 3: (0, XHALF)}[dy]
+
+        def add(o):
+            at = pl.ds(start + o, 32)
+            ysend[k, at] = (summed(k, at) + xfrecv[dy, at].astype(f32)).astype(bf16)
+        looped(size, 32, add)
+        if dy == 2:
+            for way, where in enumerate(ways):
+                one_x[way] = send(ysend.at[k, pl.ds(way * XHALF, XHALF)], y1x.at[way], where)
+        else:
+            way = 0 if dy == 1 else 1
+            two_x[way, 1] = send(ysend.at[k, pl.ds(start, XHALF)], y2recv.at[way, 0, pl.ds(start, XHALF)], ways[way])
+
+    def crossed_accumulate():
+        for way, dy in ((0, 1), (1, 3)):
+            k = ORDER.index((dy, 0))
+            one_x[way].wait_recv()
+            start = way * XHALF
+
+            def add(o):
+                at = pl.ds(start + o, 32)
+                ysend[k, at] = (summed(k, at) + xfrecv[dy, at].astype(f32)
+                                + y1x[way, pl.ds(o, 32)].astype(f32)).astype(bf16)
+            looped(XHALF, 32, add)
+            two_x[way, 0] = send(ysend.at[k, pl.ds(start, XHALF)], y2recv.at[way, 0, pl.ds(start, XHALF)], ways[way])
 
     for k in range(8):
         compute(k)
         if k >= 1:
             post(k - 1)
-        if k == 6:
+        if k == 4:
             accumulate(1)
+        if k == 5:
+            crossed(2)
     post(7)
     accumulate(0)
+    crossed(1)
+    crossed(3)
 
     crossing = []
     for part in range(2):
-        o0 = part * HALF
+        o0 = XROWS + part * HALF
         for way in range(2):
             step_two[way, 1, 0 if way == part else 1].wait_recv()
 
         def add(o):
             at = pl.ds(o0 + o, 32)
-            xsend[at] = (own[6, at] + y2recv[0, 1, at].astype(f32) + y2recv[1, 1, at].astype(f32)).astype(bf16)
+            xsend[pl.ds(part * HALF + o, 32)] = (
+                summed(6, at) + y2recv[0, 1, at].astype(f32) + y2recv[1, 1, at].astype(f32)).astype(bf16)
         looped(HALF, 32, add)
-        crossing.append(send(xsend.at[pl.ds(o0, HALF)], xrecv.at[pl.ds(o0, HALF)], across))
+        crossing.append(send(xsend.at[pl.ds(part * HALF, HALF)], xrecv.at[pl.ds(part * HALF, HALF)], across))
+        if part == 0:
+            crossed_accumulate()
     for load in late:
         load.wait()
+
+    def adam(at, far):
+        grad = summed(7, at) + y2recv[0, 0, at].astype(f32) + y2recv[1, 0, at].astype(f32) + far
+        new_m = beta_one * mbuf[at] + (1.0 - beta_one) * grad
+        new_v = beta_two * vbuf[at] + (1.0 - beta_two) * grad * grad
+        mbuf[at] = new_m
+        vbuf[at] = new_v
+        dbuf[at] = new_m / (1.0 - beta_one**20) / (jnp.sqrt(new_v / (1.0 - beta_two**20)) + epsilon)
+
     stores = []
+    first_x[0].wait_recv()
+    for way in range(2):
+        for part in range(2):
+            two_x[way, part].wait_recv()
+    looped(XROWS, 16, lambda o: adam(pl.ds(o, 16), xfrecv[0, pl.ds(o, 16)].astype(f32)))
     for part in range(2):
-        o0 = part * HALF
         for way in range(2):
             step_two[way, 0, 0 if way == part else 1].wait_recv()
         crossing[part].wait_recv()
-
-        def adam(o):
-            at = pl.ds(o0 + o, 16)
-            grad = (own[7, at] + y2recv[0, 0, at].astype(f32) + y2recv[1, 0, at].astype(f32)
-                    + xrecv[at].astype(f32))
-            new_m = beta_one * mbuf[at] + (1.0 - beta_one) * grad
-            new_v = beta_two * vbuf[at] + (1.0 - beta_two) * grad * grad
-            mbuf[at] = new_m
-            vbuf[at] = new_v
-            dbuf[at] = new_m / (1.0 - beta_one**20) / (jnp.sqrt(new_v / (1.0 - beta_two**20)) + epsilon)
-        looped(HALF, 16, adam)
+        o0 = part * HALF
+        looped(HALF, 16, lambda o: adam(pl.ds(XROWS + o0 + o, 16), xrecv[pl.ds(o0 + o, 16)].astype(f32)))
     for i, (src, dst) in enumerate(((mbuf, new_first), (vbuf, new_second))):
         store = pltpu.make_async_copy(src, dst, lsem.at[i])
         store.start()
@@ -380,12 +425,13 @@
         store.wait()
 
 
-def rebuild(basis, coeffs, first, second, rebuilt, new_first, new_second, bbuf, cbuf, obuf, sem):
+def rebuild(basis, coeffs, first, second, rebuilt, new_first, new_second, bbuf, cbuf, obuf, state, sem):
     copies = [pltpu.make_async_copy(basis, bbuf, sem.at[2])]
     copies += [pltpu.make_async_copy(coeffs.at[:, pl.ds(i * 1280, 1280)], cbuf.at[i], sem.at[3 + i]) for i in range(4)]
-    kept = [pltpu.make_async_copy(first, new_first, sem.at[0]), pltpu.make_async_copy(second, new_second, sem.at[1])]
-    for copy in copies + kept:
+    moved = [pltpu.make_async_copy(first, state.at[0], sem.at[0]), pltpu.make_async_copy(second, state.at[1], sem.at[1])]
+    for copy in copies + moved:
         copy.start()
+    kept = []
     copies[0].wait()
     for i in range(4):
         copies[1 + i].wait()
@@ -394,6 +440,11 @@
             rows = pl.ds(j * ROWS, ROWS)
             obuf[i, rows] = jnp.dot(bbuf[rows], cbuf[i], preferred_element_type=f32).astype(bf16)
             copy = pltpu.make_async_copy(obuf.at[i, rows], rebuilt.at[rows, columns], sem.at[7 + 2 * i + j])
+            copy.start()
+            kept.append(copy)
+        if i < 2:
+            moved[i].wait()
+            copy = pltpu.make_async_copy(state.at[i], (new_first, new_second)[i], sem.at[i])
             copy.start()
             kept.append(copy)
     for copy in kept:
@@ -422,9 +473,12 @@
             pltpu.VMEM((8, ROWS, COLS), bf16),
             pltpu.VMEM((6, ROWS, COLS), bf16),
             pltpu.VMEM((2, 2, HALF, COLS), bf16),
+            pltpu.VMEM((2, XHALF, COLS), bf16),
             pltpu.VMEM((2, 2, ROWS, COLS), bf16),
-            pltpu.VMEM((ROWS, COLS), bf16),
-            pltpu.VMEM((ROWS, COLS), bf16),
+            pltpu.VMEM((4, XROWS, COLS), bf16),
+            pltpu.VMEM((4, XROWS, COLS), bf16),
+            pltpu.VMEM((2 * HALF, COLS), bf16),
+            pltpu.VMEM((2 * HALF, COLS), bf16),
             pltpu.VMEM((ROWS, COLS), f32),
             pltpu.VMEM((ROWS, COLS), f32),
             pltpu.VMEM((ROWS, COLS), f32),
@@ -459,6 +513,7 @@
             pltpu.VMEM((2 * ROWS, RANK), bf16),
             pltpu.VMEM((4, RANK, 1280), bf16),
             pltpu.VMEM((4, COLS, 1280), bf16),
+            pltpu.VMEM((2, ROWS, COLS), f32),
             pltpu.SemaphoreType.DMA((15,)),
         ],
         compiler_params=pltpu.CompilerParams(vmem_limit_bytes=60 << 20),

time: 157 us -> 99.2 us (0.63)
  Pallas kernels: 156 us -> 98.3 us
    pallas_call x1, Pallas kernels: 50.9 us -> 4.84 us  [local(): pl.pallas_call(rebuild, name='rebuild', out_shape=(jax.ShapeDtypeStruct((...]
    pallas_call x1, Pallas kernels: 105 us -> 93.4 us  [local(): pl.pallas_call(kernel, name='step', out_shape=(state, state, jax.ShapeDty...]
where the time goes in v3:
time: 99.2 us; the launch traced here: 99.1 us
  Pallas kernels  98.3 us (99%)
    pallas_call x1, Pallas kernels, local(): pl.pallas_call(kernel, name='step', out_shape=(state, state, jax.ShapeDty...  93.4 us
    pallas_call x1, Pallas kernels, local(): pl.pallas_call(rebuild, name='rebuild', out_shape=(jax.ShapeDtypeStruct((...  4.84 us

profile of v3, /device:TPU:1, one launch (start us, length us, event | category | flops | bytes accessed | tf_op | source)
XLA Modules:
  0.0 99.1 jit_solution(8308035880271228647)
XLA Ops:
  0.6 93.4 %step.1 = (f32[320,640]{1,0:T(8,128)}, f32[320,640]{1,0:T(8,128)}, bf16[128,5120]{1,0:T(8,128)(2,1)}, bf16[640,128]{1,0:T(8,128)(2,1)}) custom-call(bf16[1024,5120]{1,0:T(8,128)(2,1)} %act.1, bf16[1024,640]{1,0:T(8,128)(2,1)} %cot.1, f32[320,640]{1,0:T(8,128)} %first.1, f32[320,640]{1,0:T(8,128)} %second.1, f32[640,128]{1,0:T(8,128)} %sketch.1), custom_call_target="tpu_custom_call" | custom-call | tf_op jit(solution)/shard_map/step/pallas_call | solution.py:457
  94.1 4.8 %rebuild.1 = (bf16[640,5120]{1,0:T(8,128)(2,1)}, f32[320,640]{1,0:T(8,128)}, f32[320,640]{1,0:T(8,128)}) custom-call(bf16[640,128]{1,0:T(8,128)(2,1)} %get-tuple-element.10.basis, bf16[128,5120]{1,0:T(8,128)(2,1)} %get-tuple-element.11.coeffs, f32[320,640]{1,0:T(8,128)} %get-tuple-element.12.first, f32[320,640]{1,0:T(8,128)} %get-tuple-element.13.second), custom_call_target="tpu_custom_call" | custom-call | tf_op jit(solution)/shard_map/rebuild/pallas_call | solution.py:506

commit v4 on v3

--- a/solution.py
+++ b/solution.py
@@ -44,31 +44,52 @@
     lane = lax.broadcasted_iota(jnp.int32, (8, 128), 1)
     sub = lax.broadcasted_iota(jnp.int32, (8, 128), 0)
     panels = [gram_ref[8 * i:8 * i + 8, :] for i in range(16)]
+
+    def down(v, j):
+        return jnp.broadcast_to(v[j:j + 1, :], (8, 128))
+
     for k in range(16):
         panel = panels[k]
+        last = k == 15
+        cols = [jnp.broadcast_to(panel[:, 8 * k + j:8 * k + j + 1], (8, 128)) for j in range(8)]
+        if not last:
+            ahead = panels[k + 1]
+            acols = [jnp.broadcast_to(ahead[:, 8 * k + j:8 * k + j + 1], (8, 128)) for j in range(8)]
         scale = jnp.zeros((8, 128), f32)
+        amul = []
         for j in range(8):
             p = 8 * k + j
-            col = jnp.broadcast_to(panel[:, p:p + 1], (8, 128))
-            pivot = jnp.broadcast_to(col[j:j + 1, :], (8, 128))
-            recip = 1.0 / pivot
+            recip = 1.0 / down(cols[j], j)
             scale = jnp.where(sub == j, recip, scale)
-            m = jnp.where(sub > j, -col * recip, 0.0)
-            row = jnp.broadcast_to(jnp.where(lane[j:j + 1] == p, 1.0, panel[j:j + 1, :]), (8, 128))
+            m = jnp.where(sub > j, -cols[j] * recip, 0.0)
+            row = down(jnp.where(lane == p, 1.0, panel), j)
             panel = jnp.where((lane == p) & (sub > j), 0.0, panel) + m * row
+            if not last:
+                am = -acols[j] * recip
+                amul.append(am)
+            for i in range(j + 1, 8):
+                u = down(cols[j], i)
+                cols[i] = cols[i] + m * u
+                if not last:
+                    acols[i] = acols[i] + am * u
         panels[k] = panel
-        if k < 15:
+        if not last:
             inside = (lane >= 8 * k) & (lane < 8 * k + 8)
             ext = jnp.where(inside & (lane - 8 * k > sub), 0.0, panel)
             ext = jnp.where(inside & (lane - 8 * k == sub), 1.0, ext)
-            lhs = -panel * scale
-            a1, a2, a3 = split3(lhs)
-            b1, b2, b3 = split3(ext)
-            left = jnp.concatenate([a1, a1, a2, a2, a1, a3], axis=0).astype(bf16)
-            right = jnp.concatenate([b1, b2, b1, b2, b3, b1], axis=0).astype(bf16)
-            upd = lax.dot_general(left, right, DN0, preferred_element_type=f32)
-            for i in range(k + 1, 16):
-                panels[i] = jnp.where(inside, 0.0, panels[i]) + upd[8 * i:8 * i + 8, :]
+            ahead = jnp.where(inside, 0.0, ahead)
+            for j in range(8):
+                ahead = ahead + amul[j] * down(ext, j)
+            panels[k + 1] = ahead
+            if k < 14:
+                lhs = -panel * scale
+                a1, a2, a3 = split3(lhs)
+                b1, b2, b3 = split3(ext)
+                left = jnp.concatenate([a1, a1, a2, a2, a1, a3], axis=0).astype(bf16)
+                right = jnp.concatenate([b1, b2, b1, b2, b3, b1], axis=0).astype(bf16)
+                upd = lax.dot_general(left, right, DN0, preferred_element_type=f32)
+                for i in range(k + 2, 16):
+                    panels[i] = jnp.where(inside, 0.0, panels[i]) + upd[8 * i:8 * i + 8, :]
         yield k
     for k in range(16):
         at = lane == sub + 8 * k
@@ -82,7 +103,7 @@
     new_first, new_second, coeffs_out, basis_out,
     abuf, cbuf, pbuf, own, psend, crecv, ysend, y1recv, y1x, y2recv, xfsend, xfrecv, xsend, xrecv,
     mbuf, vbuf, dbuf, skbuf, rpart, rrecv, rfull, r_out, gpart, gcrecv, gslots, gfull,
-    spart, screcv, sslots, s_out, inverse,
+    spart, screcv, sslots, s_own, inverse,
     lsem, ssem, rsem,
 ):
     f, r = lax.axis_index("fsdp"), lax.axis_index("roll")
@@ -328,15 +349,17 @@
     my_rows = pl.ds(pl.multiple_of(c * 64 + q * 8, 8), 8)
     gpart[...] = lax.dot_general(rfull[...], rfull[...], DN0, precision=hp, preferred_element_type=f32)
     gcopy = send(gpart.at[other_half], gcrecv, sibling)
-    spart[...] = lax.dot_general(rfull[...], dbuf[...], DN0, precision=hp, preferred_element_type=f32)
-    scopy = send(spart.at[other_half], screcv, sibling)
-
-    def scatter(mine, slots):
+    spart[...] = lax.dot_general(dbuf[...], rfull[...], DN0, precision=hp, preferred_element_type=f32)
+    scopy = send(spart.at[pl.ds(theirs, ROWS)], screcv, sibling)
+
+    def scatter(part, slots, rows):
+        def piece(i):
+            return pl.ds(pl.multiple_of((c * 8 + i) * rows, 8), rows)
         sent = []
         for k in range(1, 8):
             where, other = chip(k)
-            sent.append(send(mine.at[pl.ds(pl.multiple_of(c * 64 + other * 8, 8), 8)], slots.at[q], where))
-        slots[q] = mine[my_rows]
+            sent.append(send(part.at[piece(other)], slots.at[q], where))
+        slots[q] = part[piece(q)]
         return sent
 
     def gathered(sent, slots):
@@ -349,10 +372,10 @@
 
     gcopy.wait_recv()
     gpart[my_half] = gpart[my_half] + gcrecv[...]
-    gsent = scatter(gpart, gslots)
+    gsent = scatter(gpart, gslots, 8)
     scopy.wait_recv()
-    spart[my_half] = spart[my_half] + screcv[...]
-    ssent = scatter(spart, sslots)
+    spart[pl.ds(mine, ROWS)] = spart[pl.ds(mine, ROWS)] + screcv[...]
+    ssent = scatter(spart, sslots, PIECE)
     gfull[my_rows] = gathered(gsent, gslots)
     gsent = [send(gfull.at[my_rows], gfull.at[my_rows], chip(k)[0]) for k in range(1, 8)]
 
@@ -362,9 +385,9 @@
     rsent = [send(r_out.at[c, own_piece], r_out.at[c, own_piece], chip(k)[0]) for k in range(1, 8)]
 
     s, t = c * y + (1 - c) * z, c * z + (1 - c) * y
-    row = pl.ds(pl.multiple_of(xh * 8, 8), 8)
-    s_out[c, s, t, xl, row] = gathered(ssent, sslots)
-    ssent = [send(s_out.at[c, s, t, xl, row], s_out.at[c, s, t, xl, row], around_x(k)) for k in range(1, 4)]
+    at = pl.ds(pl.multiple_of(xh * PIECE, 8), PIECE)
+    s_own[t, xl, at] = gathered(ssent, sslots)
+    ssent = [send(s_own.at[t, xl, at], s_own.at[t, xl, at], around_x(k)) for k in range(1, 4)]
     for part in gsent:
         part.wait_recv()
     gcopy = send(gfull.at[my_half], gfull.at[my_half], sibling)
@@ -377,43 +400,33 @@
 
     gcopy.wait_recv()
     steps = factor_inverse(gfull, inverse)
-    next(steps)
-    for part in ssent:
-        part.wait_recv()
-    ssent = [send(s_out.at[c, s, t], s_out.at[c, s, t], along_t(k)) for k in (1, 3, 2)]
     for _ in range(4):
         next(steps)
     for part in ssent:
         part.wait_recv()
-    ssent = [send(s_out.at[c, s], s_out.at[c, s], along_s(k)) for k in (1, 3, 2)]
-    copies = [send(s_out.at[c, s], s_out.at[c, s], sibling)]
-    for _ in range(2):
-        next(steps)
-    for part in rsent:
-        part.wait_recv()
-    rcopy = send(r_out.at[c], r_out.at[c], sibling)
-    for k, part in zip((1, 3, 2), ssent):
-        for _ in range(3):
-            next(steps)
-        part.wait_recv()
-        have = (s + 4 - k) % 4
-        copies.append(send(s_out.at[c, have], s_out.at[c, have], sibling))
+    ssent = [send(s_own.at[t], s_own.at[t], along_t(k)) for k in (1, 3, 2)]
     for _ in steps:
         pass
+    for part in rsent:
+        part.wait_recv()
+    rcopy = send(r_out.at[c], r_out.at[c], sibling)
+    for part in ssent:
+        part.wait_recv()
+    coeffs = lax.dot_general(
+        s_own[...].reshape(COLS, RANK), inverse[...], DN1, precision=hp, preferred_element_type=f32)
+    coeffs_out[c, s] = coeffs.reshape(4, 2, 2 * PIECE, RANK).astype(bf16)
+    ssent = [send(coeffs_out.at[c, s], coeffs_out.at[c, s], along_s(k)) for k in (1, 3, 2)]
+    copies = [send(coeffs_out.at[c, s], coeffs_out.at[c, s], sibling)]
     rcopy.wait_recv()
     for core in range(2):
         basis_out[core * ROWS:(core + 1) * ROWS] = lax.dot_general(
             r_out[core], inverse[...], DN1, precision=hp, preferred_element_type=f32).astype(bf16)
+    for k, part in zip((1, 3, 2), ssent):
+        part.wait_recv()
+        have = (s + 4 - k) % 4
+        copies.append(send(coeffs_out.at[c, have], coeffs_out.at[c, have], sibling))
     for part in copies:
         part.wait_recv()
-
-    def block(i, carry):
-        bz, bxl = i // 2, i % 2
-        rows = [s_out[0, bz, by, bxl] for by in range(4)] + [s_out[1, by, bz, bxl] for by in range(4)]
-        coeffs_out[:, pl.ds(pl.multiple_of(i * COLS, COLS), COLS)] = jnp.dot(
-            inverse[...], jnp.concatenate(rows, axis=0), precision=hp, preferred_element_type=f32).astype(bf16)
-        return carry
-    lax.fori_loop(0, 8, block, 0)
 
     for part in pending:
         part.wait_send()
@@ -427,7 +440,8 @@
 
 def rebuild(basis, coeffs, first, second, rebuilt, new_first, new_second, bbuf, cbuf, obuf, state, sem):
     copies = [pltpu.make_async_copy(basis, bbuf, sem.at[2])]
-    copies += [pltpu.make_async_copy(coeffs.at[:, pl.ds(i * 1280, 1280)], cbuf.at[i], sem.at[3 + i]) for i in range(4)]
+    copies += [pltpu.make_async_copy(coeffs.at[0, i], cbuf.at[i, 0], sem.at[3 + i]) for i in range(4)]
+    copies += [pltpu.make_async_copy(coeffs.at[1, :, i], cbuf.at[i, 1], sem.at[15 + i]) for i in range(4)]
     moved = [pltpu.make_async_copy(first, state.at[0], sem.at[0]), pltpu.make_async_copy(second, state.at[1], sem.at[1])]
     for copy in copies + moved:
         copy.start()
@@ -435,11 +449,11 @@
     copies[0].wait()
     for i in range(4):
         copies[1 + i].wait()
-        columns = pl.ds(i * 1280, 1280)
+        copies[5 + i].wait()
         for j in range(2):
-            rows = pl.ds(j * ROWS, ROWS)
-            obuf[i, rows] = jnp.dot(bbuf[rows], cbuf[i], preferred_element_type=f32).astype(bf16)
-            copy = pltpu.make_async_copy(obuf.at[i, rows], rebuilt.at[rows, columns], sem.at[7 + 2 * i + j])
+            block = jnp.concatenate([cbuf[i, core, k, j] for core in range(2) for k in range(4)], axis=0)
+            obuf[2 * i + j] = lax.dot_general(bbuf[...], block, DN1, preferred_element_type=f32).astype(bf16)
+            copy = pltpu.make_async_copy(obuf.at[2 * i + j], rebuilt.at[:, pl.ds((2 * i + j) * COLS, COLS)], sem.at[7 + 2 * i + j])
             copy.start()
             kept.append(copy)
         if i < 2:
@@ -459,7 +473,7 @@
         name="step",
         out_shape=(
             state, state,
-            jax.ShapeDtypeStruct((RANK, D), bf16),
+            jax.ShapeDtypeStruct((2, 4, 4, 2, 2 * PIECE, RANK), bf16),
             jax.ShapeDtypeStruct((2 * ROWS, RANK), bf16),
         ),
         in_specs=[hbm] * 5,
@@ -491,10 +505,10 @@
             pltpu.VMEM((64, RANK), f32),
             pltpu.VMEM((8, 8, RANK), f32),
             pltpu.VMEM((RANK, RANK), f32),
-            pltpu.VMEM((RANK, COLS), f32),
-            pltpu.VMEM((64, COLS), f32),
-            pltpu.VMEM((8, 8, COLS), f32),
-            pltpu.VMEM((2, 4, 4, 2, 16, COLS), f32),
+            pltpu.VMEM((COLS, RANK), f32),
+            pltpu.VMEM((ROWS, RANK), f32),
+            pltpu.VMEM((8, PIECE, RANK), f32),
+            pltpu.VMEM((4, 2, 2 * PIECE, RANK), f32),
             pltpu.VMEM((RANK, RANK), f32),
             pltpu.SemaphoreType.DMA((12,)),
             pltpu.SemaphoreType.DMA((SEMS,)),
@@ -511,10 +525,10 @@
         out_specs=(hbm,) * 3,
         scratch_shapes=[
             pltpu.VMEM((2 * ROWS, RANK), bf16),
-            pltpu.VMEM((4, RANK, 1280), bf16),
-            pltpu.VMEM((4, COLS, 1280), bf16),
+            pltpu.VMEM((4, 2, 4, 2, 2 * PIECE, RANK), bf16),
+            pltpu.VMEM((8, COLS, COLS), bf16),
             pltpu.VMEM((2, ROWS, COLS), f32),
-            pltpu.SemaphoreType.DMA((15,)),
+            pltpu.SemaphoreType.DMA((19,)),
         ],
         compiler_params=pltpu.CompilerParams(vmem_limit_bytes=60 << 20),
     )(basis, coeffs, first, second)

time: 99.2 us -> 84 us (0.85)
  Pallas kernels: 98.3 us -> 83.1 us
    pallas_call x1, Pallas kernels: 93.4 us -> 77.9 us  [local(): pl.pallas_call(kernel, name='step', out_shape=(state, state, jax.ShapeDty...]
where the time goes in v4:
time: 84 us; the launch traced here: 83.9 us
  Pallas kernels  83.1 us (99%)
    pallas_call x1, Pallas kernels, local(): pl.pallas_call(kernel, name='step', out_shape=(state, state, jax.ShapeDty...  77.9 us
    pallas_call x1, Pallas kernels, local(): pl.pallas_call(rebuild, name='rebuild', out_shape=(jax.ShapeDtypeStruct((...  5.12 us

profile of v4, /device:TPU:1, one launch (start us, length us, event | category | flops | bytes accessed | tf_op | source)
XLA Modules:
  0.0 83.9 jit_solution(3473785864813887311)
XLA Ops:
  0.6 77.9 %step.1 = (f32[320,640]{1,0:T(8,128)}, f32[320,640]{1,0:T(8,128)}, bf16[2,4,4,2,80,128]{5,4,3,2,1,0:T(8,128)(2,1)}, bf16[640,128]{1,0:T(8,128)(2,1)}) custom-call(bf16[1024,5120]{1,0:T(8,128)(2,1)} %act.1, bf16[1024,640]{1,0:T(8,128)(2,1)} %cot.1, f32[320,640]{1,0:T(8,128)} %first.1, f32[320,640]{1,0:T(8,128)} %second.1, f32[640,128]{1,0:T(8,128)} %sketch.1), custom_call_target="tpu_custom_call" | custom-call | tf_op jit(solution)/shard_map/step/pallas_call | solution.py:471
  78.6 5.1 %rebuild.1 = (bf16[640,5120]{1,0:T(8,128)(2,1)}, f32[320,640]{1,0:T(8,128)}, f32[320,640]{1,0:T(8,128)}) custom-call(bf16[640,128]{1,0:T(8,128)(2,1)} %get-tuple-element.10.basis, bf16[2,4,4,2,80,128]{5,4,3,2,1,0:T(8,128)(2,1)} %get-tuple-element.11.coeffs, f32[320,640]{1,0:T(8,128)} %get-tuple-element.12.first, f32[320,640]{1,0:T(8,128)} %get-tuple-element.13.second), custom_call_target="tpu_custom_call" | custom-call | tf_op jit(solution)/shard_map/rebuild/pallas_call | solution.py:520

commit v5 on v4

--- a/solution.py
+++ b/solution.py
@@ -23,6 +23,7 @@
 XHALF = XROWS // 2
 HALF = (ROWS - XROWS) // 2
 PIECE = ROWS // 8
+FAR_FIRST = (3, 5, 4, 1, 7, 2, 6)
 
 ORDER = ((2, 1), (2, 0), (1, 1), (3, 1), (1, 0), (3, 0), (0, 1), (0, 0))
 SEMS = 112
@@ -32,7 +33,7 @@
     def one(i, carry):
         body(pl.multiple_of(i * step, step))
         return carry
-    lax.fori_loop(0, total // step, one, 0)
+    lax.fori_loop(0, total // step, one, 0, unroll=True)
 
 
 def split3(v):
@@ -148,6 +149,10 @@
         pending.append(copy)
         return copy
 
+    def drain(keep=0):
+        while len(pending) > keep:
+            pending.pop(0).wait_send()
+
     loads = []
     c_load = pltpu.make_async_copy(cot, cbuf, lsem.at[8])
     c_load.start()
@@ -320,16 +325,17 @@
 
     rpart[...] = jnp.dot(dbuf[...], skbuf[...], precision=hp, preferred_element_type=f32)
     parts = []
-    for k in range(1, 8):
+    for k in FAR_FIRST:
         where, other = roller(k)
         parts.append(send(rpart.at[pl.ds(pl.multiple_of(other * PIECE, 8), PIECE)], rrecv.at[k - 1], where))
     my_piece = pl.ds(pl.multiple_of(r * PIECE, 8), PIECE)
     total = rpart[my_piece]
+    for part in parts:
+        part.wait_recv()
     for k in range(7):
-        parts[k].wait_recv()
         total = total + rrecv[k]
     rfull[my_piece] = total
-    parts = [send(rfull.at[my_piece], rfull.at[my_piece], roller(k)[0]) for k in range(1, 8)]
+    parts = [send(rfull.at[my_piece], rfull.at[my_piece], roller(k)[0]) for k in FAR_FIRST]
     swap = remote(rfull.at[my_piece], r_out.at[c, my_piece], dev(y=z, xh=xl, z=y, xl=xh))
     own_piece = pl.ds(pl.multiple_of(q * PIECE, 8), PIECE)
     swapped = (y != z) | (xh != xl)
@@ -356,7 +362,7 @@
         def piece(i):
             return pl.ds(pl.multiple_of((c * 8 + i) * rows, 8), rows)
         sent = []
-        for k in range(1, 8):
+        for k in FAR_FIRST:
             where, other = chip(k)
             sent.append(send(part.at[piece(other)], slots.at[q], where))
         slots[q] = part[piece(q)]
@@ -377,20 +383,17 @@
     spart[pl.ds(mine, ROWS)] = spart[pl.ds(mine, ROWS)] + screcv[...]
     ssent = scatter(spart, sslots, PIECE)
     gfull[my_rows] = gathered(gsent, gslots)
-    gsent = [send(gfull.at[my_rows], gfull.at[my_rows], chip(k)[0]) for k in range(1, 8)]
+    gsent = [send(gfull.at[my_rows], gfull.at[my_rows], chip(k)[0]) for k in FAR_FIRST]
 
     @pl.when(swapped)
     def _():
         swap.wait_recv()
-    rsent = [send(r_out.at[c, own_piece], r_out.at[c, own_piece], chip(k)[0]) for k in range(1, 8)]
+    rsent = [send(r_out.at[c, own_piece], r_out.at[c, own_piece], chip(k)[0]) for k in FAR_FIRST]
 
     s, t = c * y + (1 - c) * z, c * z + (1 - c) * y
     at = pl.ds(pl.multiple_of(xh * PIECE, 8), PIECE)
     s_own[t, xl, at] = gathered(ssent, sslots)
-    ssent = [send(s_own.at[t, xl, at], s_own.at[t, xl, at], around_x(k)) for k in range(1, 4)]
-    for part in gsent:
-        part.wait_recv()
-    gcopy = send(gfull.at[my_half], gfull.at[my_half], sibling)
+    ssent = [send(s_own.at[t, xl, at], s_own.at[t, xl, at], around_x(k)) for k in (2, 1, 3)]
 
     def along_t(k):
         return dev(y=(y + (1 - c) * k) % 4, z=(z + c * k) % 4)
@@ -398,14 +401,15 @@
     def along_s(k):
         return dev(y=(y + c * k) % 4, z=(z + (1 - c) * k) % 4)
 
+    for part in ssent:
+        part.wait_recv()
+    ssent = [send(s_own.at[t], s_own.at[t], along_t(k)) for k in (2, 1, 3)]
+    for part in gsent:
+        part.wait_recv()
+    gcopy = send(gfull.at[my_half], gfull.at[my_half], sibling)
+    drain(12)
     gcopy.wait_recv()
-    steps = factor_inverse(gfull, inverse)
-    for _ in range(4):
-        next(steps)
-    for part in ssent:
-        part.wait_recv()
-    ssent = [send(s_own.at[t], s_own.at[t], along_t(k)) for k in (1, 3, 2)]
-    for _ in steps:
+    for _ in factor_inverse(gfull, inverse):
         pass
     for part in rsent:
         part.wait_recv()
@@ -415,27 +419,27 @@
     coeffs = lax.dot_general(
         s_own[...].reshape(COLS, RANK), inverse[...], DN1, precision=hp, preferred_element_type=f32)
     coeffs_out[c, s] = coeffs.reshape(4, 2, 2 * PIECE, RANK).astype(bf16)
-    ssent = [send(coeffs_out.at[c, s], coeffs_out.at[c, s], along_s(k)) for k in (1, 3, 2)]
+    ssent = [send(coeffs_out.at[c, s], coeffs_out.at[c, s], along_s(k)) for k in (2, 1, 3)]
     copies = [send(coeffs_out.at[c, s], coeffs_out.at[c, s], sibling)]
     rcopy.wait_recv()
     for core in range(2):
         basis_out[core * ROWS:(core + 1) * ROWS] = lax.dot_general(
             r_out[core], inverse[...], DN1, precision=hp, preferred_element_type=f32).astype(bf16)
-    for k, part in zip((1, 3, 2), ssent):
-        part.wait_recv()
-        have = (s + 4 - k) % 4
-        copies.append(send(coeffs_out.at[c, have], coeffs_out.at[c, have], sibling))
-    for part in copies:
-        part.wait_recv()
-
-    for part in pending:
-        part.wait_send()
 
     @pl.when(swapped)
     def _():
         swap.wait_send()
     for store in stores:
         store.wait()
+    drain(4)
+    for k, part in ((1, ssent[1]), (3, ssent[2]), (2, ssent[0])):
+        part.wait_recv()
+        have = (s + 4 - k) % 4
+        copies.append(send(coeffs_out.at[c, have], coeffs_out.at[c, have], sibling))
+    for part in copies:
+        part.wait_recv()
+
+    drain()
 
 
 def rebuild(basis, coeffs, first, second, rebuilt, new_first, new_second, bbuf, cbuf, obuf, state, sem):

time: 84 us -> 79.6 us (0.948)
  Pallas kernels: 83.1 us -> 78.6 us
    pallas_call x1, Pallas kernels: 77.9 us -> 73.5 us  [local(): pl.pallas_call(kernel, name='step', out_shape=(state, state, jax.ShapeDty...]
where the time goes in v5:
time: 79.6 us; the launch traced here: 79.4 us
  Pallas kernels  78.6 us (99%)
  between operations  0.8 us (1%)
    pallas_call x1, Pallas kernels, local(): pl.pallas_call(kernel, name='step', out_shape=(state, state, jax.ShapeDty...  73.5 us
    pallas_call x1, Pallas kernels, local(): pl.pallas_call(rebuild, name='rebuild', out_shape=(jax.ShapeDtypeStruct((...  5.11 us

profile of v5, /device:TPU:1, one launch (start us, length us, event | category | flops | bytes accessed | tf_op | source)
XLA Modules:
  0.0 79.4 jit_solution(13531601404999742835)
XLA Ops:
  0.6 73.5 %step.1 = (f32[320,640]{1,0:T(8,128)}, f32[320,640]{1,0:T(8,128)}, bf16[2,4,4,2,80,128]{5,4,3,2,1,0:T(8,128)(2,1)}, bf16[640,128]{1,0:T(8,128)(2,1)}) custom-call(bf16[1024,5120]{1,0:T(8,128)(2,1)} %act.1, bf16[1024,640]{1,0:T(8,128)(2,1)} %cot.1, f32[320,640]{1,0:T(8,128)} %first.1, f32[320,640]{1,0:T(8,128)} %second.1, f32[640,128]{1,0:T(8,128)} %sketch.1), custom_call_target="tpu_custom_call" | custom-call | tf_op jit(solution)/shard_map/step/pallas_call | solution.py:475
  74.2 5.1 %rebuild.1 = (bf16[640,5120]{1,0:T(8,128)(2,1)}, f32[320,640]{1,0:T(8,128)}, f32[320,640]{1,0:T(8,128)}) custom-call(bf16[640,128]{1,0:T(8,128)(2,1)} %get-tuple-element.10.basis, bf16[2,4,4,2,80,128]{5,4,3,2,1,0:T(8,128)(2,1)} %get-tuple-element.11.coeffs, f32[320,640]{1,0:T(8,128)} %get-tuple-element.12.first, f32[320,640]{1,0:T(8,128)} %get-tuple-element.13.second), custom_call_target="tpu_custom_call" | custom-call | tf_op jit(solution)/shard_map/rebuild/pallas_call | solution.py:524

commit v6 on v5

--- a/solution.py
+++ b/solution.py
@@ -15,6 +15,7 @@
 f32, bf16 = jnp.float32, jnp.bfloat16
 DN0 = (((0,), (0,)), ((), ()))
 DN1 = (((1,), (1,)), ((), ()))
+DN = (((1,), (0,)), ((), ()))
 
 D, TOK, RANK = 5120, 1024, 128
 COLS = 640
@@ -24,9 +25,28 @@
 HALF = (ROWS - XROWS) // 2
 PIECE = ROWS // 8
 FAR_FIRST = (3, 5, 4, 1, 7, 2, 6)
-
-ORDER = ((2, 1), (2, 0), (1, 1), (3, 1), (1, 0), (3, 0), (0, 1), (0, 0))
-SEMS = 112
+PLANE = ((2, 2), (1, 2), (3, 2), (2, 1), (2, 3), (1, 1), (3, 3), (1, 3), (3, 1), (2, 0), (0, 2), (1, 0), (3, 0), (0, 1), (0, 3))
+
+ORDER = ((2, 1), (2, 0), (1, 1), (3, 1), (0, 1), (1, 0), (3, 0), (0, 0))
+SEMS = 128
+
+
+def split(v, parts):
+    out = []
+    for _ in range(parts):
+        out.append(v.astype(bf16))
+        v = v - out[-1].astype(f32)
+    return out
+
+
+def full_dot(a, b, dims):
+    def d(x, y):
+        return lax.dot_general(x, y, dims, preferred_element_type=f32)
+    a1, a2, a3 = split(a, 3)
+    b1, b2, b3 = split(b, 3)
+    pair = jnp.concatenate([b1, b2], axis=1 - dims[0][1][0])
+    u, w = d(a1, pair), d(a2, pair)
+    return u[:, :RANK] + ((u[:, RANK:] + w[:, :RANK]) + (w[:, RANK:] + (d(a1, b3) + d(a3, b1))))
 
 
 def looped(total, step, body):
@@ -103,8 +123,8 @@
     act, cot, first, second, sketch,
     new_first, new_second, coeffs_out, basis_out,
     abuf, cbuf, pbuf, own, psend, crecv, ysend, y1recv, y1x, y2recv, xfsend, xfrecv, xsend, xrecv,
-    mbuf, vbuf, dbuf, skbuf, rpart, rrecv, rfull, r_out, gpart, gcrecv, gslots, gfull,
-    spart, screcv, sslots, s_own, inverse,
+    mbuf, vbuf, dbuf, skbuf, rpart, rrecv, rfull, r_out, gpart, gown, gcrecv, gslots, gchips, gfull,
+    spart, screcv, sslots, s_own, inverse, ctbuf, bbuf,
     lsem, ssem, rsem,
 ):
     f, r = lax.axis_index("fsdp"), lax.axis_index("roll")
@@ -127,9 +147,9 @@
         other = (r + k) % 8
         return {"fsdp": f, "roll": other}, other
 
-    def around_x(k):
-        other = (xh * 2 + xl + k) % 4
-        return dev(xh=other // 2, xl=other % 2)
+    def plane(kx, kt):
+        other = (xh * 2 + xl + kx) % 4
+        return dev(xh=other // 2, xl=other % 2, y=(y + (1 - c) * kt) % 4, z=(z + c * kt) % 4)
 
     used = [0]
 
@@ -172,7 +192,7 @@
         load.start()
 
     barrier = pltpu.get_barrier_semaphore()
-    greeted = [sibling] + [chip(k)[0] for k in range(1, 8)] + [roller(k)[0] for k in range(1, 8)] + [dev(xh=1 - xh, xl=1 - xl)]
+    greeted = [sibling] + [chip(k)[0] for k in range(1, 8)] + [roller(k)[0] for k in range(1, 8)] + [plane(kx, kt) for kx, kt in PLANE]
     for other in greeted:
         pl.semaphore_signal(barrier, inc=1, device_id=other, device_id_type=MESH)
     c_load.wait()
@@ -226,8 +246,8 @@
             step_two[way, dxh, 1] = send(
                 ysend.at[k, pl.ds(alone, HALF)], y2recv.at[way, dxh, pl.ds(alone, HALF)], ways[way])
 
-    def accumulate(dxh):
-        for way, dy in ((0, 1), (1, 3)):
+    def accumulate(dxh, which=(0, 1)):
+        for way, dy in ((way, (1, 3)[way]) for way in which):
             k = ORDER.index((dy, dxh))
             step_one[way, dxh].wait_recv()
             start = XROWS + way * HALF
@@ -255,8 +275,8 @@
             way = 0 if dy == 1 else 1
             two_x[way, 1] = send(ysend.at[k, pl.ds(start, XHALF)], y2recv.at[way, 0, pl.ds(start, XHALF)], ways[way])
 
-    def crossed_accumulate():
-        for way, dy in ((0, 1), (1, 3)):
+    def crossed_accumulate(which=(0, 1)):
+        for way, dy in ((way, (1, 3)[way]) for way in which):
             k = ORDER.index((dy, 0))
             one_x[way].wait_recv()
             start = way * XHALF
@@ -268,33 +288,38 @@
             looped(XHALF, 32, add)
             two_x[way, 0] = send(ysend.at[k, pl.ds(start, XHALF)], y2recv.at[way, 0, pl.ds(start, XHALF)], ways[way])
 
+    crossing = []
+
+    def cross(part):
+        o0 = XROWS + part * HALF
+        for way in range(2):
+            step_two[way, 1, 0 if way == part else 1].wait_recv()
+        k = ORDER.index((0, 1))
+
+        def add(o):
+            at = pl.ds(o0 + o, 32)
+            xsend[pl.ds(part * HALF + o, 32)] = (
+                summed(k, at) + y2recv[0, 1, at].astype(f32) + y2recv[1, 1, at].astype(f32)).astype(bf16)
+        looped(HALF, 32, add)
+        crossing.append(send(xsend.at[pl.ds(part * HALF, HALF)], xrecv.at[pl.ds(part * HALF, HALF)], across))
+
     for k in range(8):
         compute(k)
         if k >= 1:
             post(k - 1)
         if k == 4:
             accumulate(1)
-        if k == 5:
             crossed(2)
+        if k == 6:
+            accumulate(0, (0,))
+            crossed(1)
+        if k == 7:
+            accumulate(0, (1,))
+            crossed(3)
+    cross(0)
+    cross(1)
     post(7)
-    accumulate(0)
-    crossed(1)
-    crossed(3)
-
-    crossing = []
-    for part in range(2):
-        o0 = XROWS + part * HALF
-        for way in range(2):
-            step_two[way, 1, 0 if way == part else 1].wait_recv()
-
-        def add(o):
-            at = pl.ds(o0 + o, 32)
-            xsend[pl.ds(part * HALF + o, 32)] = (
-                summed(6, at) + y2recv[0, 1, at].astype(f32) + y2recv[1, 1, at].astype(f32)).astype(bf16)
-        looped(HALF, 32, add)
-        crossing.append(send(xsend.at[pl.ds(part * HALF, HALF)], xrecv.at[pl.ds(part * HALF, HALF)], across))
-        if part == 0:
-            crossed_accumulate()
+    crossed_accumulate()
     for load in late:
         load.wait()
 
@@ -304,7 +329,8 @@
         new_v = beta_two * vbuf[at] + (1.0 - beta_two) * grad * grad
         mbuf[at] = new_m
         vbuf[at] = new_v
-        dbuf[at] = new_m / (1.0 - beta_one**20) / (jnp.sqrt(new_v / (1.0 - beta_two**20)) + epsilon)
+        dbuf[at] = (new_m * (1.0 / (1.0 - beta_one**20))) / (
+            jnp.sqrt(new_v * (1.0 / (1.0 - beta_two**20))) + epsilon)
 
     stores = []
     first_x[0].wait_recv()
@@ -312,18 +338,21 @@
         for part in range(2):
             two_x[way, part].wait_recv()
     looped(XROWS, 16, lambda o: adam(pl.ds(o, 16), xfrecv[0, pl.ds(o, 16)].astype(f32)))
+
+    def sketched(o, n):
+        rpart[o:o + n] = full_dot(dbuf[o:o + n], skbuf[...], DN)
     for part in range(2):
         for way in range(2):
             step_two[way, 0, 0 if way == part else 1].wait_recv()
         crossing[part].wait_recv()
-        o0 = part * HALF
-        looped(HALF, 16, lambda o: adam(pl.ds(XROWS + o0 + o, 16), xrecv[pl.ds(o0 + o, 16)].astype(f32)))
+    sketched(0, XROWS)
+    looped(2 * HALF, 16, lambda o: adam(pl.ds(XROWS + o, 16), xrecv[pl.ds(o, 16)].astype(f32)))
+    sketched(XROWS, ROWS - XROWS)
     for i, (src, dst) in enumerate(((mbuf, new_first), (vbuf, new_second))):
         store = pltpu.make_async_copy(src, dst, lsem.at[i])
         store.start()
         stores.append(store)
 
-    rpart[...] = jnp.dot(dbuf[...], skbuf[...], precision=hp, preferred_element_type=f32)
     parts = []
     for k in FAR_FIRST:
         where, other = roller(k)
@@ -347,26 +376,6 @@
     @pl.when(jnp.logical_not(swapped))
     def _():
         r_out[c, own_piece] = rfull[my_piece]
-    for part in parts:
-        part.wait_recv()
-
-    my_half = pl.ds(pl.multiple_of(c * 64, 64), 64)
-    other_half = pl.ds(pl.multiple_of((1 - c) * 64, 64), 64)
-    my_rows = pl.ds(pl.multiple_of(c * 64 + q * 8, 8), 8)
-    gpart[...] = lax.dot_general(rfull[...], rfull[...], DN0, precision=hp, preferred_element_type=f32)
-    gcopy = send(gpart.at[other_half], gcrecv, sibling)
-    spart[...] = lax.dot_general(dbuf[...], rfull[...], DN0, precision=hp, preferred_element_type=f32)
-    scopy = send(spart.at[pl.ds(theirs, ROWS)], screcv, sibling)
-
-    def scatter(part, slots, rows):
-        def piece(i):
-            return pl.ds(pl.multiple_of((c * 8 + i) * rows, 8), rows)
-        sent = []
-        for k in FAR_FIRST:
-            where, other = chip(k)
-            sent.append(send(part.at[piece(other)], slots.at[q], where))
-        slots[q] = part[piece(q)]
-        return sent
 
     def gathered(sent, slots):
         for part in sent:
@@ -376,14 +385,37 @@
             total = total + slots[k]
         return total
 
+    def scatter(part, slots, peer, me, piece):
+        sent = []
+        for k in FAR_FIRST:
+            where, other = peer(k)
+            sent.append(send(part.at[piece(other)], slots.at[me], where))
+        slots[me] = part[piece(me)]
+        return sent
+
+    def sixteen(i):
+        return pl.ds(pl.multiple_of(i * 16, 16), 16)
+    piece_rows = rfull[my_piece]
+    gpart[...] = lax.dot_general(piece_rows, piece_rows, DN0, precision=hp, preferred_element_type=f32)
+    gsent = scatter(gpart, gslots, roller, r, sixteen)
+
+    give_at = pl.ds(pl.multiple_of((1 - c) * 256, 128), 384)
+    keep_at = pl.ds(pl.multiple_of(c * 384, 128), 256)
+    for part in parts:
+        part.wait_recv()
+    spart[give_at] = full_dot(dbuf[:, give_at], rfull[...], DN0)
+    scopy = send(spart.at[pl.ds(theirs, ROWS)], screcv, sibling)
+    gown[...] = gathered(gsent, gslots)
+    gcopy = send(gown, gcrecv, sibling)
+    spart[keep_at] = full_dot(dbuf[:, keep_at], rfull[...], DN0)
     gcopy.wait_recv()
-    gpart[my_half] = gpart[my_half] + gcrecv[...]
-    gsent = scatter(gpart, gslots, 8)
+    gchips[q] = gown[...] + gcrecv[...]
+    gsent = [send(gchips.at[q], gchips.at[q], chip(k)[0]) for k in FAR_FIRST]
     scopy.wait_recv()
     spart[pl.ds(mine, ROWS)] = spart[pl.ds(mine, ROWS)] + screcv[...]
-    ssent = scatter(spart, sslots, PIECE)
-    gfull[my_rows] = gathered(gsent, gslots)
-    gsent = [send(gfull.at[my_rows], gfull.at[my_rows], chip(k)[0]) for k in FAR_FIRST]
+    ssent = scatter(spart, sslots, chip, q, lambda i: pl.ds(pl.multiple_of((c * 8 + i) * PIECE, 8), PIECE))
+    gfull[sixteen(r)] = gathered(gsent, gchips)
+    gsent = [send(gfull.at[sixteen(r)], gfull.at[sixteen(r)], roller(k)[0]) for k in FAR_FIRST]
 
     @pl.when(swapped)
     def _():
@@ -393,22 +425,14 @@
     s, t = c * y + (1 - c) * z, c * z + (1 - c) * y
     at = pl.ds(pl.multiple_of(xh * PIECE, 8), PIECE)
     s_own[t, xl, at] = gathered(ssent, sslots)
-    ssent = [send(s_own.at[t, xl, at], s_own.at[t, xl, at], around_x(k)) for k in (2, 1, 3)]
-
-    def along_t(k):
-        return dev(y=(y + (1 - c) * k) % 4, z=(z + c * k) % 4)
+    ssent = [send(s_own.at[t, xl, at], s_own.at[t, xl, at], plane(kx, kt)) for kx, kt in PLANE]
 
     def along_s(k):
         return dev(y=(y + c * k) % 4, z=(z + (1 - c) * k) % 4)
 
-    for part in ssent:
-        part.wait_recv()
-    ssent = [send(s_own.at[t], s_own.at[t], along_t(k)) for k in (2, 1, 3)]
     for part in gsent:
         part.wait_recv()
-    gcopy = send(gfull.at[my_half], gfull.at[my_half], sibling)
-    drain(12)
-    gcopy.wait_recv()
+    drain(16)
     for _ in factor_inverse(gfull, inverse):
         pass
     for part in rsent:
@@ -416,29 +440,37 @@
     rcopy = send(r_out.at[c], r_out.at[c], sibling)
     for part in ssent:
         part.wait_recv()
-    coeffs = lax.dot_general(
-        s_own[...].reshape(COLS, RANK), inverse[...], DN1, precision=hp, preferred_element_type=f32)
-    coeffs_out[c, s] = coeffs.reshape(4, 2, 2 * PIECE, RANK).astype(bf16)
-    ssent = [send(coeffs_out.at[c, s], coeffs_out.at[c, s], along_s(k)) for k in (2, 1, 3)]
-    copies = [send(coeffs_out.at[c, s], coeffs_out.at[c, s], sibling)]
+    coeffs = full_dot(s_own[...].reshape(COLS, RANK), inverse[...], DN1)
+    ctbuf[c, s] = coeffs.reshape(4, 2, 2 * PIECE, RANK).astype(bf16)
+    ssent = [send(ctbuf.at[c, s], ctbuf.at[c, s], along_s(k)) for k in (2, 1, 3)]
+    copies = [send(ctbuf.at[c, s], ctbuf.at[c, s], sibling)]
+
+    def keep(core, place, i):
+        store = pltpu.make_async_copy(ctbuf.at[core, place], coeffs_out.at[core, place], lsem.at[i])
+        store.start()
+        stores.append(store)
+    keep(c, s, 2)
     rcopy.wait_recv()
     for core in range(2):
-        basis_out[core * ROWS:(core + 1) * ROWS] = lax.dot_general(
-            r_out[core], inverse[...], DN1, precision=hp, preferred_element_type=f32).astype(bf16)
+        bbuf[core * ROWS:(core + 1) * ROWS] = full_dot(r_out[core], inverse[...], DN1).astype(bf16)
+    stores.append(pltpu.make_async_copy(bbuf, basis_out, lsem.at[3]))
+    stores[-1].start()
 
     @pl.when(swapped)
     def _():
         swap.wait_send()
+    drain(4)
+    for i, (k, part) in enumerate(((1, ssent[1]), (3, ssent[2]), (2, ssent[0]))):
+        part.wait_recv()
+        have = (s + 4 - k) % 4
+        copies.append(send(ctbuf.at[c, have], ctbuf.at[c, have], sibling))
+        keep(c, have, 4 + i)
+    theirs_s = c * z + (1 - c) * y
+    for i, k in enumerate((0, 1, 3, 2)):
+        copies[i].wait_recv()
+        keep(1 - c, (theirs_s + 4 - k) % 4, 7 + i)
     for store in stores:
         store.wait()
-    drain(4)
-    for k, part in ((1, ssent[1]), (3, ssent[2]), (2, ssent[0])):
-        part.wait_recv()
-        have = (s + 4 - k) % 4
-        copies.append(send(coeffs_out.at[c, have], coeffs_out.at[c, have], sibling))
-    for part in copies:
-        part.wait_recv()
-
     drain()
 
 
@@ -470,7 +502,7 @@
 
 
 def local(activations, cotangent, first_moment, second_moment, sketch):
-    hbm, vmem = pl.BlockSpec(memory_space=pltpu.HBM), pl.BlockSpec(memory_space=pltpu.VMEM)
+    hbm = pl.BlockSpec(memory_space=pltpu.HBM)
     state = jax.ShapeDtypeStruct((ROWS, COLS), f32)
     first, second, coeffs, basis = pl.pallas_call(
         kernel,
@@ -481,7 +513,7 @@
             jax.ShapeDtypeStruct((2 * ROWS, RANK), bf16),
         ),
         in_specs=[hbm] * 5,
-        out_specs=(hbm, hbm, vmem, vmem),
+        out_specs=(hbm,) * 4,
         scratch_shapes=[
             pltpu.VMEM((8, TOK, 640), bf16),
             pltpu.VMEM((TOK, COLS), bf16),
@@ -489,7 +521,7 @@
             pltpu.VMEM((8, ROWS, COLS), f32),
             pltpu.VMEM((8, ROWS, COLS), bf16),
             pltpu.VMEM((8, ROWS, COLS), bf16),
-            pltpu.VMEM((6, ROWS, COLS), bf16),
+            pltpu.VMEM((7, ROWS, COLS), bf16),
             pltpu.VMEM((2, 2, HALF, COLS), bf16),
             pltpu.VMEM((2, XHALF, COLS), bf16),
             pltpu.VMEM((2, 2, ROWS, COLS), bf16),
@@ -506,14 +538,18 @@
             pltpu.VMEM((ROWS, RANK), f32),
             pltpu.VMEM((2, ROWS, RANK), f32),
             pltpu.VMEM((RANK, RANK), f32),
-            pltpu.VMEM((64, RANK), f32),
-            pltpu.VMEM((8, 8, RANK), f32),
+            pltpu.VMEM((16, RANK), f32),
+            pltpu.VMEM((16, RANK), f32),
+            pltpu.VMEM((8, 16, RANK), f32),
+            pltpu.VMEM((8, 16, RANK), f32),
             pltpu.VMEM((RANK, RANK), f32),
             pltpu.VMEM((COLS, RANK), f32),
             pltpu.VMEM((ROWS, RANK), f32),
             pltpu.VMEM((8, PIECE, RANK), f32),
             pltpu.VMEM((4, 2, 2 * PIECE, RANK), f32),
             pltpu.VMEM((RANK, RANK), f32),
+            pltpu.VMEM((2, 4, 4, 2, 2 * PIECE, RANK), bf16),
+            pltpu.VMEM((2 * ROWS, RANK), bf16),
             pltpu.SemaphoreType.DMA((12,)),
             pltpu.SemaphoreType.DMA((SEMS,)),
             pltpu.SemaphoreType.DMA((SEMS,)),

time: 79.6 us -> 77.3 us (0.971)
  Pallas kernels: 78.6 us -> 76.4 us
    pallas_call x1, Pallas kernels: 73.5 us -> 71.3 us  [local(): pl.pallas_call(kernel, name='step', out_shape=(state, state, jax.ShapeDty...]
where the time goes in v6:
time: 77.3 us; the launch traced here: 77.2 us
  Pallas kernels  76.4 us (99%)
  between operations  0.8 us (1%)
    pallas_call x1, Pallas kernels, local(): pl.pallas_call(kernel, name='step', out_shape=(state, state, jax.ShapeDty...  71.3 us
    pallas_call x1, Pallas kernels, local(): pl.pallas_call(rebuild, name='rebuild', out_shape=(jax.ShapeDtypeStruct((...  5.11 us

profile of v6, /device:TPU:1, one launch (start us, length us, event | category | flops | bytes accessed | tf_op | source)
XLA Modules:
  0.0 77.2 jit_solution(374920761477380969)
XLA Ops:
  0.6 71.3 %step.1 = (f32[320,640]{1,0:T(8,128)}, f32[320,640]{1,0:T(8,128)}, bf16[2,4,4,2,80,128]{5,4,3,2,1,0:T(8,128)(2,1)}, bf16[640,128]{1,0:T(8,128)(2,1)}) custom-call(bf16[1024,5120]{1,0:T(8,128)(2,1)} %act.1, bf16[1024,640]{1,0:T(8,128)(2,1)} %cot.1, f32[320,640]{1,0:T(8,128)} %first.1, f32[320,640]{1,0:T(8,128)} %second.1, f32[640,128]{1,0:T(8,128)} %sketch.1), custom_call_target="tpu_custom_call" | custom-call | tf_op jit(solution)/shard_map/step/pallas_call | solution.py:507
  71.9 5.1 %rebuild.1 = (bf16[640,5120]{1,0:T(8,128)(2,1)}, f32[320,640]{1,0:T(8,128)}, f32[320,640]{1,0:T(8,128)}) custom-call(bf16[640,128]{1,0:T(8,128)(2,1)} %get-tuple-element.10.basis, bf16[2,4,4,2,80,128]{5,4,3,2,1,0:T(8,128)(2,1)} %get-tuple-element.11.coeffs, f32[320,640]{1,0:T(8,128)} %get-tuple-element.12.first, f32[320,640]{1,0:T(8,128)} %get-tuple-element.13.second), custom_call_target="tpu_custom_call" | custom-call | tf_op jit(solution)/shard_map/rebuild/pallas_call | solution.py:560

commit v7 on v6

--- a/solution.py
+++ b/solution.py
@@ -417,10 +417,6 @@
     gfull[sixteen(r)] = gathered(gsent, gchips)
     gsent = [send(gfull.at[sixteen(r)], gfull.at[sixteen(r)], roller(k)[0]) for k in FAR_FIRST]
 
-    @pl.when(swapped)
-    def _():
-        swap.wait_recv()
-    rsent = [send(r_out.at[c, own_piece], r_out.at[c, own_piece], chip(k)[0]) for k in FAR_FIRST]
 
     s, t = c * y + (1 - c) * z, c * z + (1 - c) * y
     at = pl.ds(pl.multiple_of(xh * PIECE, 8), PIECE)
@@ -435,9 +431,10 @@
     drain(16)
     for _ in factor_inverse(gfull, inverse):
         pass
-    for part in rsent:
-        part.wait_recv()
-    rcopy = send(r_out.at[c], r_out.at[c], sibling)
+    @pl.when(swapped)
+    def _():
+        swap.wait_recv()
+    rsent = [send(r_out.at[c, own_piece], r_out.at[c, own_piece], chip(k)[0]) for k in FAR_FIRST]
     for part in ssent:
         part.wait_recv()
     coeffs = full_dot(s_own[...].reshape(COLS, RANK), inverse[...], DN1)
@@ -450,6 +447,9 @@
         store.start()
         stores.append(store)
     keep(c, s, 2)
+    for part in rsent:
+        part.wait_recv()
+    rcopy = send(r_out.at[c], r_out.at[c], sibling)
     rcopy.wait_recv()
     for core in range(2):
         bbuf[core * ROWS:(core + 1) * ROWS] = full_dot(r_out[core], inverse[...], DN1).astype(bf16)

time: 77.3 us -> 76.5 us (0.990)
  Pallas kernels: 76.4 us -> 75.5 us
    pallas_call x1, Pallas kernels: 71.3 us -> 70.4 us  [local(): pl.pallas_call(kernel, name='step', out_shape=(state, state, jax.ShapeDty...]
where the time goes in v7:
time: 76.5 us; the launch traced here: 76.3 us
  Pallas kernels  75.5 us (99%)
  between operations  0.8 us (1%)
    pallas_call x1, Pallas kernels, local(): pl.pallas_call(kernel, name='step', out_shape=(state, state, jax.ShapeDty...  70.4 us
    pallas_call x1, Pallas kernels, local(): pl.pallas_call(rebuild, name='rebuild', out_shape=(jax.ShapeDtypeStruct((...  5.12 us

profile of v7, /device:TPU:1, one launch (start us, length us, event | category | flops | bytes accessed | tf_op | source)
XLA Modules:
  0.0 76.3 jit_solution(12328677823972744991)
XLA Ops:
  0.6 70.4 %step.1 = (f32[320,640]{1,0:T(8,128)}, f32[320,640]{1,0:T(8,128)}, bf16[2,4,4,2,80,128]{5,4,3,2,1,0:T(8,128)(2,1)}, bf16[640,128]{1,0:T(8,128)(2,1)}) custom-call(bf16[1024,5120]{1,0:T(8,128)(2,1)} %act.1, bf16[1024,640]{1,0:T(8,128)(2,1)} %cot.1, f32[320,640]{1,0:T(8,128)} %first.1, f32[320,640]{1,0:T(8,128)} %second.1, f32[640,128]{1,0:T(8,128)} %sketch.1), custom_call_target="tpu_custom_call" | custom-call | tf_op jit(solution)/shard_map/step/pallas_call | solution.py:507
  71.1 5.1 %rebuild.1 = (bf16[640,5120]{1,0:T(8,128)(2,1)}, f32[320,640]{1,0:T(8,128)}, f32[320,640]{1,0:T(8,128)}) custom-call(bf16[640,128]{1,0:T(8,128)(2,1)} %get-tuple-element.10.basis, bf16[2,4,4,2,80,128]{5,4,3,2,1,0:T(8,128)(2,1)} %get-tuple-element.11.coeffs, f32[320,640]{1,0:T(8,128)} %get-tuple-element.12.first, f32[320,640]{1,0:T(8,128)} %get-tuple-element.13.second), custom_call_target="tpu_custom_call" | custom-call | tf_op jit(solution)/shard_map/rebuild/pallas_call | solution.py:560

commit v8 on v7

--- a/solution.py
+++ b/solution.py
@@ -345,9 +345,10 @@
         for way in range(2):
             step_two[way, 0, 0 if way == part else 1].wait_recv()
         crossing[part].wait_recv()
-    sketched(0, XROWS)
-    looped(2 * HALF, 16, lambda o: adam(pl.ds(XROWS + o, 16), xrecv[pl.ds(o, 16)].astype(f32)))
-    sketched(XROWS, ROWS - XROWS)
+        o0 = part * HALF
+        sketched(*((0, XROWS) if part == 0 else (XROWS, HALF)))
+        looped(HALF, 16, lambda o: adam(pl.ds(XROWS + o0 + o, 16), xrecv[pl.ds(o0 + o, 16)].astype(f32)))
+    sketched(XROWS + HALF, HALF)
     for i, (src, dst) in enumerate(((mbuf, new_first), (vbuf, new_second))):
         store = pltpu.make_async_copy(src, dst, lsem.at[i])
         store.start()
@@ -492,11 +493,12 @@
             copy = pltpu.make_async_copy(obuf.at[2 * i + j], rebuilt.at[:, pl.ds((2 * i + j) * COLS, COLS)], sem.at[7 + 2 * i + j])
             copy.start()
             kept.append(copy)
-        if i < 2:
-            moved[i].wait()
-            copy = pltpu.make_async_copy(state.at[i], (new_first, new_second)[i], sem.at[i])
-            copy.start()
-            kept.append(copy)
+        if i == 1:
+            for j, kept_state in enumerate((new_first, new_second)):
+                moved[j].wait()
+                copy = pltpu.make_async_copy(state.at[j], kept_state, sem.at[j])
+                copy.start()
+                kept.append(copy)
     for copy in kept:
         copy.wait()
 

time: 76.5 us -> 76.8 us (level)
  no operation moved by 1% of the time
where the time goes in v8:
time: 76.8 us; the launch traced here: 76.7 us
  Pallas kernels  75.9 us (99%)
  between operations  0.8 us (1%)
    pallas_call x1, Pallas kernels, local(): pl.pallas_call(kernel, name='step', out_shape=(state, state, jax.ShapeDty...  70.7 us
    pallas_call x1, Pallas kernels, local(): pl.pallas_call(rebuild, name='rebuild', out_shape=(jax.ShapeDtypeStruct((...  5.18 us

profile of v8, /device:TPU:1, one launch (start us, length us, event | category | flops | bytes accessed | tf_op | source)
XLA Modules:
  0.0 76.7 jit_solution(14946098642898234045)
XLA Ops:
  0.6 70.7 %step.1 = (f32[320,640]{1,0:T(8,128)}, f32[320,640]{1,0:T(8,128)}, bf16[2,4,4,2,80,128]{5,4,3,2,1,0:T(8,128)(2,1)}, bf16[640,128]{1,0:T(8,128)(2,1)}) custom-call(bf16[1024,5120]{1,0:T(8,128)(2,1)} %act.1, bf16[1024,640]{1,0:T(8,128)(2,1)} %cot.1, f32[320,640]{1,0:T(8,128)} %first.1, f32[320,640]{1,0:T(8,128)} %second.1, f32[640,128]{1,0:T(8,128)} %sketch.1), custom_call_target="tpu_custom_call" | custom-call | tf_op jit(solution)/shard_map/step/pallas_call | solution.py:509
  71.3 5.2 %rebuild.1 = (bf16[640,5120]{1,0:T(8,128)(2,1)}, f32[320,640]{1,0:T(8,128)}, f32[320,640]{1,0:T(8,128)}) custom-call(bf16[640,128]{1,0:T(8,128)(2,1)} %get-tuple-element.10.basis, bf16[2,4,4,2,80,128]{5,4,3,2,1,0:T(8,128)(2,1)} %get-tuple-element.11.coeffs, f32[320,640]{1,0:T(8,128)} %get-tuple-element.12.first, f32[320,640]{1,0:T(8,128)} %get-tuple-element.13.second), custom_call_target="tpu_custom_call" | custom-call | tf_op jit(solution)/shard_map/rebuild/pallas_call | solution.py:562

commit v9 on v7

--- a/solution.py
+++ b/solution.py
@@ -431,10 +431,6 @@
     drain(16)
     for _ in factor_inverse(gfull, inverse):
         pass
-    @pl.when(swapped)
-    def _():
-        swap.wait_recv()
-    rsent = [send(r_out.at[c, own_piece], r_out.at[c, own_piece], chip(k)[0]) for k in FAR_FIRST]
     for part in ssent:
         part.wait_recv()
     coeffs = full_dot(s_own[...].reshape(COLS, RANK), inverse[...], DN1)
@@ -447,24 +443,29 @@
         store.start()
         stores.append(store)
     keep(c, s, 2)
-    for part in rsent:
+    @pl.when(swapped)
+    def _():
+        swap.wait_recv()
+    rsent = [send(r_out.at[c, own_piece], r_out.at[c, own_piece], chip(k)[0]) for k in FAR_FIRST]
+
+    @pl.when(swapped)
+    def _():
+        swap.wait_send()
+    drain(11)
+    for i, (k, part) in enumerate(((1, ssent[1]), (3, ssent[2]), (2, ssent[0]))):
         part.wait_recv()
-    rcopy = send(r_out.at[c], r_out.at[c], sibling)
+        have = (s + 4 - k) % 4
+        copies.append(send(ctbuf.at[c, have], ctbuf.at[c, have], sibling))
+        keep(c, have, 4 + i)
+        if k == 3:
+            for part in rsent:
+                part.wait_recv()
+            rcopy = send(r_out.at[c], r_out.at[c], sibling)
     rcopy.wait_recv()
     for core in range(2):
         bbuf[core * ROWS:(core + 1) * ROWS] = full_dot(r_out[core], inverse[...], DN1).astype(bf16)
     stores.append(pltpu.make_async_copy(bbuf, basis_out, lsem.at[3]))
     stores[-1].start()
-
-    @pl.when(swapped)
-    def _():
-        swap.wait_send()
-    drain(4)
-    for i, (k, part) in enumerate(((1, ssent[1]), (3, ssent[2]), (2, ssent[0]))):
-        part.wait_recv()
-        have = (s + 4 - k) % 4
-        copies.append(send(ctbuf.at[c, have], ctbuf.at[c, have], sibling))
-        keep(c, have, 4 + i)
     theirs_s = c * z + (1 - c) * y
     for i, k in enumerate((0, 1, 3, 2)):
         copies[i].wait_recv()

time: 76.5 us -> 77.2 us (level)
  Pallas kernels: 75.5 us -> 76.3 us
where the time goes in v9:
time: 77.2 us; the launch traced here: 77.1 us
  Pallas kernels  76.3 us (99%)
  between operations  0.8 us (1%)
    pallas_call x1, Pallas kernels, local(): pl.pallas_call(kernel, name='step', out_shape=(state, state, jax.ShapeDty...  71.2 us
    pallas_call x1, Pallas kernels, local(): pl.pallas_call(rebuild, name='rebuild', out_shape=(jax.ShapeDtypeStruct((...  5.12 us

profile of v9, /device:TPU:1, one launch (start us, length us, event | category | flops | bytes accessed | tf_op | source)
XLA Modules:
  0.0 77.1 jit_solution(3211372231886313192)
XLA Ops:
  0.6 71.2 %step.1 = (f32[320,640]{1,0:T(8,128)}, f32[320,640]{1,0:T(8,128)}, bf16[2,4,4,2,80,128]{5,4,3,2,1,0:T(8,128)(2,1)}, bf16[640,128]{1,0:T(8,128)(2,1)}) custom-call(bf16[1024,5120]{1,0:T(8,128)(2,1)} %act.1, bf16[1024,640]{1,0:T(8,128)(2,1)} %cot.1, f32[320,640]{1,0:T(8,128)} %first.1, f32[320,640]{1,0:T(8,128)} %second.1, f32[640,128]{1,0:T(8,128)} %sketch.1), custom_call_target="tpu_custom_call" | custom-call | tf_op jit(solution)/shard_map/step/pallas_call | solution.py:508
  71.8 5.1 %rebuild.1 = (bf16[640,5120]{1,0:T(8,128)(2,1)}, f32[320,640]{1,0:T(8,128)}, f32[320,640]{1,0:T(8,128)}) custom-call(bf16[640,128]{1,0:T(8,128)(2,1)} %get-tuple-element.10.basis, bf16[2,4,4,2,80,128]{5,4,3,2,1,0:T(8,128)(2,1)} %get-tuple-element.11.coeffs, f32[320,640]{1,0:T(8,128)} %get-tuple-element.12.first, f32[320,640]{1,0:T(8,128)} %get-tuple-element.13.second), custom_call_target="tpu_custom_call" | custom-call | tf_op jit(solution)/shard_map/rebuild/pallas_call | solution.py:561
